TPU v7x, 512 devices: a whole 4x8x8 slice. The times are simulated.
512 devices in a mesh: own: 32 (over y, x), dp: 16 (over z, core).
Axes of the slice: x: 4, y: 8, z: 8, core: 2. Of those that a mesh axis runs over, the one named last changes fastest.
Arguments:
- acts: bfloat16 [4096, 2048], P('own', 'dp'), may hold values from -6 to 6
- grads_out: bfloat16 [4096, 15360], P('own', 'dp'), may hold values from -0.09375 to 0.09375
- stats: float32 [32, 16, 1, 512, 512], P('own', 'dp'), as said below
- owner: int32 [120, 1], replicated, may hold values from 0 to 31; in each aligned block of 30 rows (0 to 29, 30 to 59, ...) at most 2 rows name the same one
- col_index: int32 [4, 30], replicated, may hold values from 0 to 29, each once within a row
Outputs:
- update: bfloat16 [32, 16, 2, 128, 512], P('own', 'dp')
Inputs may be any that keep to these rules, and one draw needn't show every extreme that they name: Within one block-row (aligned runs of 30 entries) no owner holds more than 2 blocks, and in some block-row an owner holds exactly 2. `col_index`: each row is a permutation. `stats`: each matrix is symmetric, and each diagonal entry exceeds the sum of magnitudes of the other entries of its row.
All inputs are finite; a program needn't handle non-finite values.
Results may differ from a plain program's by a relative error of at most 0.028.
Values may be sent and summed in bfloat16 or wider, within the bound.
A program may use at most 64 MiB of HBM per device.

v0:
```python
import jax
import jax.numpy as jnp
from jax import lax
from jax.sharding import PartitionSpec as P

STAT_DECAY = 0.9
EPSILON = 1e-06


def partner_2(x, axis, distance):
    return lax.ppermute(x, axis, [(i, i ^ 1 << distance) for i in range(lax.axis_size(axis))])


def exact_product(left, right):
    return jnp.einsum("sij,sjk->sik", left, right, precision=lax.Precision.HIGHEST)


def inverse_roots(matrices):
    size = matrices.shape[-1]
    identity = jnp.eye(size, dtype=jnp.float32)
    scale = jnp.trace(matrices, axis1=1, axis2=2) / size + EPSILON
    start = matrices / scale[:, None, None]
    first = (5.0 * identity - start) / 4.0
    square = exact_product(first, first)
    fourth = exact_product(square, square)
    moved = exact_product(fourth, start)
    second = (5.0 * identity - moved) / 4.0
    return exact_product(first, second)


def shards(acts, grads_out, stats, owner, col_index):
    own_size = lax.axis_size("own")
    dp_pos = lax.axis_index("dp")
    group_size = 4
    block_row = dp_pos // group_size
    quarter = dp_pos % group_size
    quarter_rows = acts.shape[1]
    block_size = group_size * quarter_rows
    per_device = stats.shape[2]
    capacity = 2 * per_device
    piece_rows = quarter_rows // own_size
    cotangents = lax.all_gather(grads_out, "dp", axis=1, tiled=True)
    width = cotangents.shape[1]
    row_blocks = width // block_size
    row_owner = lax.dynamic_slice_in_dim(owner[:, 0], block_row * row_blocks, row_blocks)
    row_columns = lax.dynamic_index_in_dim(col_index, block_row, 0, keepdims=False)
    positions = jnp.arange(row_blocks, dtype=jnp.int32)
    slot_ids = jnp.arange(capacity, dtype=jnp.int32)
    same_owner = row_owner[:, None] == row_owner[None, :]
    earlier = positions[None, :] < positions[:, None]
    slot_of = jnp.sum((same_owner & earlier).astype(jnp.int32), axis=1)
    owner_hit = (row_owner[:, None] == jnp.arange(own_size, dtype=jnp.int32)[None, :]).astype(
        jnp.float32
    )
    slot_hit = (slot_of[:, None] == slot_ids[None, :]).astype(jnp.float32)
    column_hit = (row_columns[:, None] == positions[None, :]).astype(jnp.float32)
    select = jnp.einsum("ko,ks,kp->osp", owner_hit, slot_hit, column_hit).astype(jnp.bfloat16)
    summed = lax.psum_scatter(
        jnp.einsum("ta,tb->ab", acts, cotangents, preferred_element_type=jnp.float32).astype(
            jnp.bfloat16
        ),
        "own",
        scatter_dimension=0,
        tiled=True,
    )
    pieces = summed.reshape(piece_rows, row_blocks, block_size)
    outgoing = jnp.einsum(
        "osp,rpc->osrc", select, pieces, preferred_element_type=jnp.float32
    ).astype(jnp.bfloat16)
    arrived = lax.all_to_all(outgoing, "own", split_axis=0, concat_axis=2, tiled=True)
    gradient = arrived[0]
    group_bits = group_size.bit_length() - 1
    for bit in range(group_bits):
        partner = partner_2(gradient, "dp", bit)
        upper_bit = dp_pos // (1 << bit) % 2
        gradient = jnp.where(
            upper_bit == 0,
            jnp.concatenate([gradient, partner], axis=1),
            jnp.concatenate([partner, gradient], axis=1),
        )
    side = quarter % 2
    paired = gradient.reshape(per_device, 2, block_size, block_size)
    chosen = lax.dynamic_index_in_dim(paired, quarter // 2, 1, keepdims=False)
    oriented = jnp.where(side == 0, chosen, jnp.swapaxes(chosen, 1, 2))
    products = jnp.einsum("sij,skj->sik", oriented, oriented, preferred_element_type=jnp.float32)
    updated = STAT_DECAY * stats[0, 0] + (1.0 - STAT_DECAY) * products
    factor = inverse_roots(updated).astype(jnp.bfloat16)
    collected = factor[None]
    for bit in range(group_bits):
        partner_roots = partner_2(collected, "dp", bit)
        upper_bit = dp_pos // (1 << bit) % 2
        collected = jnp.where(
            upper_bit == 0,
            jnp.concatenate([collected, partner_roots], axis=0),
            jnp.concatenate([partner_roots, collected], axis=0),
        )
    all_roots = jnp.swapaxes(collected, 0, 1).reshape(capacity, 2, block_size, block_size)
    left_roots = all_roots[:, 0]
    right_roots = all_roots[:, 1]
    wide = gradient.astype(jnp.float32)
    grad_scale = jnp.sqrt(jnp.mean(wide * wide, axis=(1, 2)) + EPSILON)
    carried = jnp.einsum(
        "sij,sjk->sik", left_roots, gradient, preferred_element_type=jnp.float32
    ).astype(jnp.bfloat16)
    whole = jnp.einsum("sij,sjk->sik", carried, right_roots, preferred_element_type=jnp.float32)
    squares = jnp.sum(whole * whole, axis=(1, 2))
    precond = lax.dynamic_slice_in_dim(whole, quarter * quarter_rows, quarter_rows, 1)
    prec_scale = jnp.sqrt(squares / (block_size * block_size) + EPSILON)
    result = precond * (grad_scale / prec_scale)[:, None, None]
    return result.astype(jnp.bfloat16)[None, None]


def solution(mesh):
    return jax.shard_map(
        shards,
        mesh=mesh,
        in_specs=(P("own", "dp"), P("own", "dp"), P("own", "dp", None, None, None), P(), P()),
        out_specs=P("own", "dp", None, None, None),
        check_vma=False,
    )
```

profile of v0, /device:TPU:1, one launch (start us, length us, event | category | flops | bytes accessed | tf_op | source)
XLA Modules:
  0.0 335.7 jit_solution(1486649641913807454)
XLA Ops:
  6.5 0.0 copy-start
  6.5 0.0 all-gather.2.cloned.1.call-start
  6.5 0.7 all-gather.2.cloned.1.call-update
  7.3 0.0 all-reduce.3.cloned.1.call-start
  7.3 53.5 %all-gather.2.cloned.1.call-done = bf16[128,15360]{0,1:T(8,128)(2,1)} async-done(((bf16[128,960]{0,1:T(8,128)(2,1)}), bf16[128,15360]{0,1:T(8,128)(2,1)}) %all-gather.2.cloned.1.call-update) | async-done | bytes 3932176 | tf_op jit(solution)/shard_map/all_gather | solution.py:42
  60.8 0.0 copy-done
  60.8 5.2 %convolution_convert_fusion = bf16[128,15360]{1,0:T(8,128)(2,1)} fusion(bf16[128,128]{1,0:T(8,128)(2,1)S(1)} %copy-done, bf16[128,15360]{0,1:T(8,128)(2,1)} %all-gather.2.cloned.1.call-done), kind=kOutput, calls=%fused_computation | convolution fusion | flops 505282560 | bytes 7897088 | tf_op jit(solution)/shard_map/ta,tb->ab/dot_general | solution.py:59
  66.0 0.0 copy-start.2
  66.0 0.0 all-reduce.3.cloned.1.call-update
  66.0 1.3 dynamic-slice.2
  67.9 0.7 fusion.33
  68.6 0.0 copy-done.2
  68.6 0.1 fusion.34
  68.7 0.2 convert_reduce_fusion
  68.9 165.0 %all-reduce.3.cloned.1.call-done = bf16[128,15360]{1,0:T(8,128)(2,1)} async-done(((bf16[128,15360]{1,0:T(8,128)(2,1)}), bf16[128,15360]{1,0:T(8,128)(2,1)}) %all-reduce.3.cloned.1.call-update) | async-done | bytes 3932176
  233.9 1.0 constant_dynamic-slice_fusion.3
  234.9 0.1 reshape.174
  235.0 0.4 convolution_convert_fusion.3
  235.4 0.2 copy.25
  235.6 15.7 %all_to_all.15 = bf16[32,2,4,512]{3,2,1,0:T(4,128)(2,1)S(1)} all-to-all(bf16[32,2,4,512]{3,2,1,0:T(4,128)(2,1)S(1)} %copy.25), channel_id=1, replica_groups=mesh['own'=32,'dp'=16] {'own'}, dimensions={0} | all-to-all | bytes 524288 | tf_op jit(solution)/shard_map/all_to_all | solution.py:70
  251.3 0.2 copy.26
  251.5 6.6 %collective-permute-start = (bf16[2,128,512]{2,0,1:T(2,128)(2,1)S(1)}, bf16[2,128,512]{2,0,1:T(2,128)(2,1)S(1)}, u32[]{:S(2)}, u32[]{:S(2)}) collective-permute-start(bf16[2,128,512]{2,0,1:T(2,128)(2,1)S(1)} %bitcast.59), channel_id=1, source_target_pairs={{0,1},{1,0},{2,3},{3,2},{4,5},{5,4},{6,7},{7,6},{8,9},{9,8},{10,11... | collective-permute-start | bytes 786440 | tf_op jit(solution)/shard_map/ppermute | solution.py:11
  258.1 1.1 collective-permute-done
  259.2 1.2 broadcast_select_fusion.2
  260.4 3.5 %collective-permute-start.1 = (bf16[2,256,512]{2,0,1:T(2,128)(2,1)S(1)}, bf16[2,256,512]{2,0,1:T(2,128)(2,1)S(1)}, u32[]{:S(2)}, u32[]{:S(2)}) collective-permute-start(bf16[2,256,512]{2,0,1:T(2,128)(2,1)S(1)} %broadcast_select_fusion.2), channel_id=1, source_target_pairs={{0,2},{1,3},{2,0},{3,1},{4,6},{5,7},{6,4},{7,5},{8,10},{9,11},{10,... | collective-permute-start | bytes 1572872 | tf_op jit(solution)/shard_map/ppermute | solution.py:11
  263.9 11.5 %collective-permute-done.1 = bf16[2,256,512]{2,0,1:T(2,128)(2,1)S(1)} collective-permute-done((bf16[2,256,512]{2,0,1:T(2,128)(2,1)S(1)}, bf16[2,256,512]{2,0,1:T(2,128)(2,1)S(1)}, u32[]{:S(2)}, u32[]{:S(2)}) %collective-permute-start.1) | collective-permute-done | bytes 524320 | tf_op jit(solution)/shard_map/ppermute | solution.py:11
  275.4 2.6 multiply_reduce_fusion.1
  278.0 1.1 constant_dynamic-slice_fusion
  279.1 2.1 copy.27
  281.2 0.0 copy-start.1
  281.2 1.6 broadcast_select_fusion.1
  282.8 0.0 copy-done.1
  282.8 1.1 select_reduce_fusion
  284.6 2.0 fusion.9
  286.6 1.8 fusion.43
  288.4 1.9 fusion.2
  290.3 2.0 fusion.3
  292.3 3.1 collective-permute-start.2
  295.4 1.5 collective-permute-done.2
  296.9 0.2 maximum_select_fusion.1
  297.1 3.3 collective-permute-start.3
  300.4 23.0 %collective-permute-done.3 = bf16[2,1,512,512]{3,2,1,0:T(8,128)(2,1)S(1)} collective-permute-done((bf16[2,1,512,512]{3,2,1,0:T(8,128)(2,1)S(1)}, bf16[2,1,512,512]{3,2,1,0:T(8,128)(2,1)S(1)}, u32[]{:S(2)}, u32[]{:S(2)}) %collective-permute-start.3) | collective-permute-done | bytes 1048608 | tf_op jit(solution)/shard_map/ppermute | solution.py:11
  323.3 1.7 maximum_select_fusion
  325.0 3.0 multiply_reduce_fusion
  328.0 0.8 fusion.19
  (3 shorter events, 0.0 us)
Async XLA Ops:
  6.5 54.2 %copy-start = (bf16[128,128]{1,0:T(8,128)(2,1)S(1)}, bf16[128,128]{1,0:T(8,128)(2,1)}, u32[]{:S(2)}) copy-start(bf16[128,128]{1,0:T(8,128)(2,1)} %param.5) | copy-start | bytes 98308
  6.5 54.2 %all-gather.2.cloned.1.call-start = ((), (), s32[]{:S(2)}) async-start(), calls=%async_computation.1 | async-start | bytes 4177920 | tf_op jit(solution)/shard_map/all_gather | solution.py:42
  7.3 226.6 %all-reduce.3.cloned.1.call-start = ((), (), s32[]{:S(2)}) async-start(), calls=%async_computation.2 | async-start | bytes 7864320
  66.0 2.7 copy-start.2
  251.5 7.7 %collective-permute-start = (bf16[2,128,512]{2,0,1:T(2,128)(2,1)S(1)}, bf16[2,128,512]{2,0,1:T(2,128)(2,1)S(1)}, u32[]{:S(2)}, u32[]{:S(2)}) collective-permute-start(bf16[2,128,512]{2,0,1:T(2,128)(2,1)S(1)} %bitcast.59), channel_id=1, source_target_pairs={{0,1},{1,0},{2,3},{3,2},{4,5},{5,4},{6,7},{7,6},{8,9},{9,8},{10,11... | collective-permute-start | bytes 786440 | tf_op jit(solution)/shard_map/ppermute | solution.py:11
  260.4 15.0 %collective-permute-start.1 = (bf16[2,256,512]{2,0,1:T(2,128)(2,1)S(1)}, bf16[2,256,512]{2,0,1:T(2,128)(2,1)S(1)}, u32[]{:S(2)}, u32[]{:S(2)}) collective-permute-start(bf16[2,256,512]{2,0,1:T(2,128)(2,1)S(1)} %broadcast_select_fusion.2), channel_id=1, source_target_pairs={{0,2},{1,3},{2,0},{3,1},{4,6},{5,7},{6,4},{7,5},{8,10},{9,11},{10,... | collective-permute-start | bytes 1572872 | tf_op jit(solution)/shard_map/ppermute | solution.py:11
  281.2 1.6 copy-start.1
  292.3 4.6 %collective-permute-start.2 = (bf16[1,1,512,512]{3,2,1,0:T(8,128)(2,1)S(1)}, bf16[1,1,512,512]{3,2,1,0:T(8,128)(2,1)S(1)}, u32[]{:S(2)}, u32[]{:S(2)}) collective-permute-start(bf16[1,1,512,512]{3,2,1,0:T(8,128)(2,1)S(1)} %fusion.3), channel_id=1, source_target_pairs={{0,1},{1,0},{2,3},{3,2},{4,5},{5,4},{6,7},{7,6},{8,9},{9,8},{10,11... | collective-permute-start | bytes 1572872 | tf_op jit(solution)/shard_map/ppermute | solution.py:11
  297.1 26.3 %collective-permute-start.3 = (bf16[2,1,512,512]{3,2,1,0:T(8,128)(2,1)S(1)}, bf16[2,1,512,512]{3,2,1,0:T(8,128)(2,1)S(1)}, u32[]{:S(2)}, u32[]{:S(2)}) collective-permute-start(bf16[2,1,512,512]{3,2,1,0:T(8,128)(2,1)S(1)} %maximum_select_fusion.1), channel_id=1, source_target_pairs={{0,2},{1,3},{2,0},{3,1},{4,6},{5,7},{6,4},{7,5},{8,10},{9,11},{10,... | collective-permute-start | bytes 3145736 | tf_op jit(solution)/shard_map/ppermute | solution.py:11
Sparse Core Ops, SparseCore 0:
  9.5 51.2 all-gather.1
  66.1 167.7 all-reduce.2
where the time goes:
time: 336 us
  waiting for transfers between devices  256 us (76%)
  matrix products  17.4 us (5%)
  starting transfers between devices  16.5 us (5%)
  blocking collectives  15.7 us (5%)
  between operations  15 us (4%)
  other arithmetic  8.21 us (2%)
  local copies, waits for them, and re-layouts  6.73 us (2%)
    unnamed x3, waiting for transfers between devices  166 us
    all_gather x1, waiting for transfers between devices, shards(): cotangents = lax.all_gather(grads_out, 'dp', axis=1, tiled=True)  53.5 us
    ppermute x4, waiting for transfers between devices, partner_2(): lax.ppermute(x, axis, [(i, i ^ 1 << distance) for i in range(lax.axis_siz...  37.1 us
    ppermute x4, starting transfers between devices, partner_2(): lax.ppermute(x, axis, [(i, i ^ 1 << distance) for i in range(lax.axis_siz...  16.4 us
    all_to_all x1, blocking collectives, shards(): lax.all_to_all(outgoing, 'own', split_axis=0, concat_axis=2, tiled=True)  15.7 us
    dot_general x4, matrix products, exact_product(): jnp.einsum('sij,sjk->sik', left, right, precision=lax.Precision.HIGHEST)  7.64 us
  transfers between devices with their start and end apart: 6, of which 6 were waited for; matrix products, arithmetic and copies ran while one was open for 1% of the time, Pallas kernels for 0%

commit v1 on v0

v1 whole, which is shorter than its diff:
```python
import jax
import jax.numpy as jnp
from jax import lax
from jax.experimental import pallas as pl
from jax.experimental.pallas import tpu as pltpu
from jax.sharding import PartitionSpec as P

STAT_DECAY = 0.9
EPSILON = 1e-06
MESH = pl.DeviceIdType.MESH
BF = jnp.bfloat16
F32 = jnp.float32
NX, NY, NZ = 4, 8, 8
NE = 2 * NZ
BS = 512
TOK = 128
COLS = 960
HALF = 240
NB = 30
SLOTS = 64
NN = (((1,), (0,)), ((), ()))
NT = (((1,), (1,)), ((), ()))
TN = (((0,), (0,)), ((), ()))


def dot(a, b, dims=NN):
    return lax.dot_general(a, b, dims, preferred_element_type=F32)


def split(a):
    high = a.astype(BF)
    return high, (a - high.astype(F32)).astype(BF)


def exact_product(a, b):
    (ah, al), (bh, bl) = a, b
    return dot(ah, bh) + (dot(ah, bl) + dot(al, bh))


def wait(ref, sem):
    pltpu.make_async_copy(ref, ref, sem).wait()


def kernel(
    tab, acts, grads, stats, out,
    bt, am, part, snd, rcv, summed, tiles, outgoing, h4, rt, stat, work, res, got,
    b_send, b_recv, a_send, a_recv, f_send, f_recv, r_send, r_recv, t_send, t_recv,
    o_send, o_recv, h_send, h_recv, q_send, q_recv, u_send, u_recv, s_sem,
):
    own = lax.axis_index("own")
    dp = lax.axis_index("dp")
    y, x = lax.div(own, NX), lax.rem(own, NX)
    z, c = lax.div(dp, 2), lax.rem(dp, 2)
    brow, side = lax.div(z, 2), lax.rem(z, 2)
    sibling = (own, dp + 1 - 2 * c)
    pair = (own, dp + 2 - 4 * side)

    def ring(step):
        return lax.rem(y + step + NY, NY)

    def remote(src, dst, send_sem, recv_sem, device):
        return pltpu.make_async_remote_copy(
            src_ref=src, dst_ref=dst, send_sem=send_sem, recv_sem=recv_sem,
            device_id=device, device_id_type=MESH,
        )

    stat_copy = pltpu.make_async_copy(stats, stat, s_sem)
    stat_copy.start()

    barrier = pltpu.get_barrier_semaphore()

    def greet(device):
        pl.semaphore_signal(barrier, inc=1, device_id=device, device_id_type=MESH)

    for i in range(1, NX):
        greet((y * NX + lax.rem(x + i, NX), dp))
    greet((ring(1) * NX + x, dp))
    greet((ring(-1) * NX + x, dp))
    for i in range(1, NE):
        greet((own, lax.rem(dp + i, NE)))
    mine = brow == x

    for i in range(NX):
        for s in range(2):
            @pl.when(jnp.logical_not(jnp.logical_and(x == i, z == 2 * x + s)))
            def _():
                greet((y * NX + i, 2 * (2 * x + s) + c))

    turned = jnp.swapaxes(grads[...].astype(F32), 0, 1).astype(BF)
    turned = turned.reshape(NB, 2, 16, TOK)
    for h in range(2):
        bt[x, pl.ds(480 * h, 480), :] = turned[:, h].reshape(480, TOK)
    tiles[NB] = jnp.zeros((16, 128), BF)

    pl.semaphore_wait(barrier, (NX - 1) + 2 + (NE - 1) + NZ - mine.astype(jnp.int32))

    b_copies = []
    for i in range(1, NX):
        copy = remote(
            bt.at[x], bt.at[x], b_send.at[i - 1], b_recv.at[x],
            (y * NX + lax.rem(x + i, NX), dp),
        )
        copy.start()
        b_copies.append(copy)

    for i in range(NZ):
        here = jnp.logical_and(mine, z == i)

        @pl.when(here)
        def _():
            pltpu.make_async_copy(acts, am.at[x, side, c], a_recv).start()

        @pl.when(jnp.logical_not(here))
        def _():
            remote(
                acts, am.at[x, side, c], a_send, a_recv, (y * NX + brow, 2 * i + c)
            ).start()

    wait(am.at[:, :, 0], a_recv)
    forward = remote(am.at[:, :, c], am.at[:, :, c], f_send, f_recv, sibling)
    forward.start()
    forward.wait_recv()
    for i in range(1, NX):
        other = lax.rem(x + i, NX)
        wait(bt.at[other], b_recv.at[other])

    right = jnp.concatenate(
        [
            jnp.concatenate([am[i, s, k] for s in range(2) for k in range(2)], axis=1)
            for i in range(NX)
        ],
        axis=0,
    )
    for h in range(2):
        left = jnp.concatenate([bt[i, pl.ds(480 * h, 480), :] for i in range(NX)], axis=1)
        product = dot(left, right)
        for k in range(4):
            part[4 * h + k] = product[:, 128 * k : 128 * k + 128]

    started = []

    def hop(way, step, half, fresh):
        sign = 1 - 2 * way
        piece = ring(sign * (4 - step))
        value = part[piece, pl.ds(HALF * half, HALF), :]
        if not fresh:
            wait(rcv.at[way, step - 1, half], r_recv.at[way, step - 1, half])
            value = value + rcv[way, step - 1, half].astype(F32)
        snd[way, step, half] = value.astype(BF)
        copy = remote(
            snd.at[way, step, half], rcv.at[way, step, half],
            r_send.at[way, step, half], r_recv.at[way, step, half],
            (ring(sign) * NX + x, dp),
        )
        copy.start()
        started.append(copy)

    for way in range(2):
        hop(way, 0, 1 - way, True)
    for way in range(2):
        hop(way, 1, way, True)
    for step in range(1, 4):
        for way in range(2):
            hop(way, step, 1 - way, False)
        if step < 3:
            for way in range(2):
                hop(way, step + 1, way, False)
    for half in range(2):
        value = part[y, pl.ds(HALF * half, HALF), :]
        for way in range(2):
            wait(rcv.at[way, 3, half], r_recv.at[way, 3, half])
            value = value + rcv[way, 3, half].astype(F32)
        summed[pl.ds(15 * half, 15)] = value.astype(BF).reshape(15, 16, 128)

    def spread(k, carry):
        place = NB * dp + k
        target = lax.rem(place, NE)
        block = lax.div(place, NE)

        @pl.when(target == dp)
        def _():
            pltpu.make_async_copy(summed.at[k], tiles.at[block], t_recv).start()

        @pl.when(target != dp)
        def _():
            remote(summed.at[k], tiles.at[block], t_send, t_recv, (own, target)).start()

        return carry

    lax.fori_loop(0, NB, spread, 0)
    wait(tiles.at[pl.ds(0, NB)], t_recv)

    lanes = pl.ds(pl.multiple_of(128 * lax.rem(y, 4), 128), 128)
    rows = pl.ds(pl.multiple_of(16 * lax.div(y, 4), 16), 16)

    def deliver(k, carry):
        owner, slot = lax.div(k, 2), lax.rem(k, 2)
        target = 2 * (2 * x + slot) + c
        outgoing[k] = tiles[tab[SLOTS * x + k]]
        here = jnp.logical_and(owner == own, target == dp)

        @pl.when(here)
        def _():
            pltpu.make_async_copy(outgoing.at[k], h4.at[z, c, rows, lanes], o_recv).start()

        @pl.when(jnp.logical_not(here))
        def _():
            remote(
                outgoing.at[k], h4.at[z, c, rows, lanes], o_send, o_recv, (owner, target)
            ).start()

        return carry

    lax.fori_loop(0, SLOTS, deliver, 0)
    wait(h4.at[:, 0], o_recv)
    swap = remote(h4.at[:, c], h4.at[:, c], h_send, h_recv, sibling)
    swap.start()
    stat_copy.wait()
    swap.wait_recv()

    block = h4[...].reshape(BS, BS)

    @pl.when(c == 0)
    def _():
        work[...] = dot(block, block, TN)

    @pl.when(c != 0)
    def _():
        work[...] = dot(block, block, NT)

    factor = STAT_DECAY * stat[...] + (1.0 - STAT_DECAY) * work[...]
    eye = lax.broadcasted_iota(jnp.int32, (BS, BS), 0) == lax.broadcasted_iota(
        jnp.int32, (BS, BS), 1
    )
    scale = jnp.sum(jnp.where(eye, factor, 0.0)) / BS + EPSILON
    first = (jnp.where(eye, 5.0, 0.0) - factor / scale) / 4.0
    pieces = split(first)
    square = exact_product(pieces, pieces)
    pieces = split(square)
    fourth = exact_product(pieces, pieces)
    moved = exact_product(split(fourth), split(5.0 * first - 4.0 * square))
    rt[c] = ((5.0 * first - moved) / 4.0).astype(BF)
    roots = remote(rt.at[c], rt.at[c], q_send, q_recv, sibling)
    roots.start()
    wide = block.astype(F32)
    grad_scale = jnp.sqrt(jnp.sum(wide * wide) / (BS * BS) + EPSILON)
    roots.wait_recv()

    carried = dot(rt[0], block, NT).astype(BF)
    whole = dot(carried, rt[1])
    prec_scale = jnp.sqrt(jnp.sum(whole * whole) / (BS * BS) + EPSILON)
    res[...] = (whole * (grad_scale / prec_scale)).astype(BF).reshape(4, 128, BS)
    last = remote(res.at[2 * (1 - side) + c], got, u_send, u_recv, pair)
    last.start()
    out[0, 0, side] = res[2 * side + c]
    last.wait_recv()
    out[0, 0, 1 - side] = got[...]

    last.wait_send()
    roots.wait_send()
    swap.wait_send()
    forward.wait_send()
    for copy in b_copies + started:
        copy.wait_send()

    @pl.when(mine)
    def _():
        wait(bt.at[0, pl.ds(0, 7 * 128)], a_send)
        wait(outgoing.at[pl.ds(0, SLOTS - 1)], o_send)

    @pl.when(jnp.logical_not(mine))
    def _():
        wait(am.at[:, :, 0], a_send)
        wait(outgoing, o_send)

    two = lax.rem(3 * dp, NE) < NB - NE

    @pl.when(two)
    def _():
        wait(summed.at[pl.ds(0, NB - 2)], t_send)

    @pl.when(jnp.logical_not(two))
    def _():
        wait(summed.at[pl.ds(0, NB - 1)], t_send)


def slot_table(owner, col_index):
    owners = owner[:, 0].reshape(col_index.shape)
    positions = jnp.arange(NB, dtype=jnp.int32)
    earlier = positions[None, :] < positions[:, None]
    same = owners[:, :, None] == owners[:, None, :]
    slot = jnp.sum((same & earlier[None]).astype(jnp.int32), axis=2)
    place = 2 * owners + slot
    hit = place[:, None, :] == jnp.arange(SLOTS, dtype=jnp.int32)[None, :, None]
    return (NB + jnp.sum(jnp.where(hit, col_index[:, None, :] - NB, 0), axis=2)).reshape(-1)


def shards(acts, grads_out, stats, owner, col_index):
    dma = pltpu.SemaphoreType.DMA
    vmem = pl.BlockSpec(memory_space=pltpu.VMEM)
    return pl.pallas_call(
        kernel,
        out_shape=jax.ShapeDtypeStruct((1, 1, 2, 128, BS), BF),
        in_specs=[
            pl.BlockSpec(memory_space=pltpu.SMEM), vmem, vmem, pl.BlockSpec(memory_space=pl.ANY)
        ],
        out_specs=vmem,
        scratch_shapes=[
            pltpu.VMEM((NX, COLS, TOK), BF),
            pltpu.VMEM((NX, 2, 2, TOK, 128), BF),
            pltpu.VMEM((NY, 2 * HALF, 128), F32),
            pltpu.VMEM((2, 4, 2, HALF, 128), BF),
            pltpu.VMEM((2, 4, 2, HALF, 128), BF),
            pltpu.VMEM((NB, 16, 128), BF),
            pltpu.VMEM((NB + 1, 16, 128), BF),
            pltpu.VMEM((SLOTS, 16, 128), BF),
            pltpu.VMEM((NZ, 2, 32, BS), BF),
            pltpu.VMEM((2, BS, BS), BF),
            pltpu.VMEM((BS, BS), F32),
            pltpu.VMEM((BS, BS), F32),
            pltpu.VMEM((4, 128, BS), BF),
            pltpu.VMEM((128, BS), BF),
            dma((NX - 1,)), dma((NX,)), dma(()), dma(()), dma(()), dma(()),
            dma((2, 4, 2)), dma((2, 4, 2)), dma(()), dma(()),
            dma(()), dma(()), dma(()), dma(()), dma(()), dma(()), dma(()), dma(()), dma(()),
        ],
        compiler_params=pltpu.CompilerParams(
            collective_id=0, has_side_effects=True, vmem_limit_bytes=48 * 1024 * 1024
        ),
    )(slot_table(owner, col_index), acts, grads_out, stats.reshape(BS, BS))


def solution(mesh):
    return jax.shard_map(
        shards,
        mesh=mesh,
        in_specs=(P("own", "dp"), P("own", "dp"), P("own", "dp", None, None, None), P(), P()),
        out_specs=P("own", "dp", None, None, None),
        check_vma=False,
    )
```

time: 336 us -> 91.6 us (0.27)
  waiting for transfers between devices: 256 us -> 0 us
  Pallas kernels: 0 us -> 84.7 us
  matrix products: 17.4 us -> 0 us
  starting transfers between devices: 16.5 us -> 0 us
  blocking collectives: 15.7 us -> 0 us
  between operations: 15 us -> 0.06 us
  other arithmetic: 8.21 us -> 1.48 us
    unnamed x3 -> x0, waiting for transfers between devices: 166 us -> none
    pallas_call x0 -> x1, Pallas kernels: none -> 84.7 us  [shards(): pl.pallas_call(kernel, out_shape=jax.ShapeDtypeStruct((1, 1, 2, 128, BS),...]
    all_gather x1 -> x0, waiting for transfers between devices: 53.5 us -> none  [shards(): cotangents = lax.all_gather(grads_out, 'dp', axis=1, tiled=True)]
    ppermute x4 -> x0, waiting for transfers between devices: 37.1 us -> none  [partner_2(): lax.ppermute(x, axis, [(i, i ^ 1 << distance) for i in range(lax.axis_siz...]
    dot_general x8 -> x0, matrix products: 17.4 us -> none  [the longest x4 7.64 us: exact_product(): jnp.einsum('sij,sjk->sik', left, right, precision=lax.Precision.HIGHEST)]
    ppermute x4 -> x0, starting transfers between devices: 16.4 us -> none  [partner_2(): lax.ppermute(x, axis, [(i, i ^ 1 << distance) for i in range(lax.axis_siz...]
    all_to_all x1 -> x0, blocking collectives: 15.7 us -> none  [shards(): lax.all_to_all(outgoing, 'own', split_axis=0, concat_axis=2, tiled=True)]
    select_n x4 -> x0, other arithmetic: 4.62 us -> none  [the longest x2 1.84 us: shards(): jnp.where(upper_bit == 0, jnp.concatenate([collected, partner_roots], axi...]
  transfers between devices with their start and end apart: 6 -> 0, of which waited for: 6 -> 0; matrix products, arithmetic and copies ran while one was open for 1% -> 0% of each run, Pallas kernels for 0% -> 0%
where the time goes in v1:
time: 91.6 us; the launch traced here: 91.1 us
  Pallas kernels  84.7 us (92%)
  local copies, waits for them, and re-layouts  4.81 us (5%)
  other arithmetic  1.48 us (2%)
    pallas_call x1, Pallas kernels, shards(): pl.pallas_call(kernel, out_shape=jax.ShapeDtypeStruct((1, 1, 2, 128, BS),...  84.7 us
    unnamed x11, local copies, waits for them, and re-layouts  4.26 us

profile of v1, /device:TPU:1, one launch (start us, length us, event | category | flops | bytes accessed | tf_op | source)
XLA Modules:
  0.0 91.1 jit_solution(6279037527336262642)
XLA Ops:
  0.0 0.0 copy-start.3
  0.0 0.5 broadcast.22
  0.5 0.1 copy-done.3
  0.7 0.7 reduce.3
  1.3 0.0 copy-start.2
  1.3 0.1 reshape_squeeze.3
  1.4 0.6 copy-done.2
  2.0 0.1 copy.14
  2.1 0.1 copy.11
  2.2 0.6 convert_reduce_fusion
  2.9 0.1 copy.12
  3.0 0.1 copy.13
  3.1 0.1 select_reduce_fusion
  3.2 0.1 add.22.tab
  3.3 0.0 copy-start.1
  3.3 1.1 %copy.15.grads = bf16[128,960]{1,0:T(8,128)(2,1)S(1)} copy(bf16[128,960]{0,1:T(8,128)(2,1)} %param.6) | data formatting | bytes 491520 | tf_op args[1]
  4.4 0.0 copy-done.1
  4.4 0.0 copy-start
  4.4 1.2 %copy-done = f32[1,1,1,512,512]{4,3,2,1,0:T(8,128)S(1)} copy-done((f32[1,1,1,512,512]{4,3,2,1,0:T(8,128)S(1)}, f32[1,1,1,512,512]{4,3,2,1,0:T(8,128)}, u32[]{:S(2)}) %copy-start) | copy-done | bytes 1048600
  5.6 84.7 %shard_map.55 = bf16[1,1,2,128,512]{4,3,2,1,0:T(8,128)(2,1)S(1)} custom-call(s32[256]{0:T(256)S(1)} %add.22.tab, bf16[128,128]{1,0:T(8,128)(2,1)S(1)} %copy-done.1, bf16[128,960]{1,0:T(8,128)(2,1)S(1)} %copy.15.grads, f32[512,512]{1,0:T(8,128)S(1)} %bitcast.2), custom_call_target="tpu_custom_call" | custom-call | tf_op jit(solution)/shard_map/pallas_call | solution.py:301
  90.4 0.7 copy.17
  (4 shorter events, 0.0 us)
Async XLA Ops:
  0.0 0.7 copy-start.3
  1.3 0.7 copy-start.2
  3.3 1.1 %copy-start.1 = (bf16[128,128]{1,0:T(8,128)(2,1)S(1)}, bf16[128,128]{1,0:T(8,128)(2,1)}, u32[]{:S(2)}) copy-start(bf16[128,128]{1,0:T(8,128)(2,1)} %acts.1) | copy-start | bytes 98308
  4.4 1.2 %copy-start = (f32[1,1,1,512,512]{4,3,2,1,0:T(8,128)S(1)}, f32[1,1,1,512,512]{4,3,2,1,0:T(8,128)}, u32[]{:S(2)}) copy-start(f32[1,1,1,512,512]{4,3,2,1,0:T(8,128)} %param.7) | copy-start | bytes 3145732

commit v2 on v1

v2 whole, which is shorter than its diff:
```python
import jax
import jax.numpy as jnp
from jax import lax
from jax.experimental import pallas as pl
from jax.experimental.pallas import tpu as pltpu
from jax.sharding import PartitionSpec as P

STAT_DECAY = 0.9
EPSILON = 1e-06
MESH = pl.DeviceIdType.MESH
BF = jnp.bfloat16
F32 = jnp.float32
NX, NY, NZ = 4, 8, 8
NE = 2 * NZ
BS = 512
TOK = 128
COLS = 960
HALF = 240
SUB = 80
HOPS = 42
NB = 30
SLOTS = 64
ORDER = sorted(
    ((i, k, s) for i in range(NY) for k in range(NX) for s in range(2)),
    key=lambda t: -min(t[0], NY - t[0]) - min(t[1], NX - t[1]),
)
NN = (((1,), (0,)), ((), ()))
NT = (((1,), (1,)), ((), ()))
TN = (((0,), (0,)), ((), ()))


def dot(a, b, dims=NN):
    return lax.dot_general(a, b, dims, preferred_element_type=F32)


def split(a):
    high = a.astype(BF)
    return high, (a - high.astype(F32)).astype(BF)


def exact_product(a, b):
    (ah, al), (bh, bl) = a, b
    return dot(ah, bh) + (dot(ah, bl) + dot(al, bh))


def wait(ref, sem):
    pltpu.make_async_copy(ref, ref, sem).wait()


def kernel(
    owner, col_index, acts, grads, stats, out,
    bt, am, part, snd, rcv, summed, tiles, outgoing, h4, rt, stat, work, res, got, slots, table,
    b_send, b_recv, a_send, a_recv, f_send, f_recv, r_send, r_recv, t_send, t_recv,
    o_send, o_recv, h_send, h_recv, q_send, q_recv, u_send, u_recv, s_sem, g_sem,
):
    own = lax.axis_index("own")
    dp = lax.axis_index("dp")
    y, x = lax.div(own, NX), lax.rem(own, NX)
    z, c = lax.div(dp, 2), lax.rem(dp, 2)
    side = lax.rem(z, 2)
    brow = lax.div(z, 2)
    crow = lax.rem(x + z, NX)
    mine = brow == crow
    spot = 2 * (4 * side + x) + c
    sibling = (own, dp + 1 - 2 * c)
    pair = (own, dp + 2 - 4 * side)

    def ring(step):
        return lax.rem(y + step + NY, NY)

    def remote(src, dst, send_sem, recv_sem, device):
        return pltpu.make_async_remote_copy(
            src_ref=src, dst_ref=dst, send_sem=send_sem, recv_sem=recv_sem,
            device_id=device, device_id_type=MESH,
        )

    pending = []

    stat_copy = pltpu.make_async_copy(stats, stat, s_sem)
    stat_copy.start()

    barrier = pltpu.get_barrier_semaphore()

    def greet(device):
        pl.semaphore_signal(barrier, inc=1, device_id=device, device_id_type=MESH)

    for i in (1, -1):
        greet((y * NX + lax.rem(x + i + NX, NX), dp))
        greet((ring(i) * NX + x, dp))
    greet(sibling)
    for i in range(NX):
        for s in range(2):
            @pl.when(jnp.logical_not(jnp.logical_and(x == i, z == 2 * crow + s)))
            def _():
                greet((y * NX + i, 2 * (2 * crow + s) + c))

    turned = grads[...].reshape(NB, 2, 16, TOK)
    for g in range(2):
        for h in range(2):
            bt[x, pl.ds(HALF * (2 * g + h), HALF), :] = turned[15 * g : 15 * g + 15, h].reshape(
                HALF, TOK
            )
    summed[...] = jnp.zeros_like(summed)
    tiles[2 * NE] = jnp.zeros((16, 128), BF)

    lane = lax.broadcasted_iota(jnp.int32, (8, 128), 1)
    none = jnp.full((8, 128), NB, jnp.int32)

    def enter(k, taken):
        hit = lane == owner[NB * brow + k]
        free = taken[0] == NB
        return (
            jnp.where(jnp.logical_and(hit, free), col_index[brow, k], taken[0]),
            jnp.where(jnp.logical_and(hit, jnp.logical_not(free)), col_index[brow, k], taken[1]),
        )

    for slot, taken in enumerate(lax.fori_loop(0, NB, enter, (none, none))):
        place = NE * taken + spot
        source = lax.shift_right_logical(place * 2185, 16)
        tile = 2 * source + lax.shift_right_logical(place - NB * source, 4)
        slots[slot] = jnp.where(taken == NB, 2 * NE, tile)
    table_copy = pltpu.make_async_copy(slots, table, g_sem)
    table_copy.start()

    pl.semaphore_wait(barrier, 5 + NZ - mine.astype(jnp.int32))

    for i in range(NZ):
        here = jnp.logical_and(mine, z == i)

        @pl.when(here)
        def _():
            pltpu.make_async_copy(acts, am.at[x, side, c], a_recv).start()

        @pl.when(jnp.logical_not(here))
        def _():
            remote(
                acts, am.at[x, side, c], a_send, a_recv,
                (y * NX + lax.rem(brow - i + 2 * NX, NX), 2 * i + c),
            ).start()

    @pending.append
    def _():
        @pl.when(mine)
        def _():
            wait(bt.at[0, pl.ds(0, 7 * 128)], a_send)

        @pl.when(jnp.logical_not(mine))
        def _():
            wait(am.at[:, :, 0], a_send)

    def pass_on(shard, g, way, kind):
        there = bt.at[shard, pl.ds(2 * HALF * g, 2 * HALF)]
        copy = remote(
            there, there, b_send.at[g, kind], b_recv.at[g, kind],
            (y * NX + lax.rem(x + (1 if way == 0 else NX - 1), NX), dp),
        )
        copy.start()
        pending.append(copy.wait_send)

    def arrive(g, kind):
        shard = lax.rem(x + (NX - 1, 1, 2)[kind], NX)
        wait(bt.at[shard, pl.ds(2 * HALF * g, 2 * HALF)], b_recv.at[g, kind])
        return shard

    for g in range(2):
        for way in range(2):
            pass_on(x, g, way, way)
    pass_on(arrive(0, 0), 0, 0, 2)
    pass_on(arrive(1, 1), 1, 1, 2)

    wait(am.at[:, :, 0], a_recv)
    forward = remote(am.at[:, :, c], am.at[:, :, c], f_send, f_recv, sibling)
    forward.start()
    pending.append(forward.wait_send)
    forward.wait_recv()
    arrive(0, 1)
    arrive(0, 2)

    right = jnp.concatenate(
        [
            jnp.concatenate([am[i, s, k] for s in range(2) for k in range(2)], axis=1)
            for i in range(NX)
        ],
        axis=0,
    )
    def multiply(g):
        for h in range(2):
            rows = pl.ds(HALF * (2 * g + h), HALF)
            left = jnp.concatenate([bt[i, rows, :] for i in range(NX)], axis=1)
            product = dot(left, right)
            for k in range(4):
                part[4 * h + k, pl.ds(HALF * g, HALF), :] = product[:, 128 * k : 128 * k + 128]

    where = {}
    for step in range(4):
        for way in range(2):
            for sub in range(6):
                if step or sub // 3 != way:
                    where[way, step, sub] = len(where)

    def hop(way, step, half, fresh):
        sign = 1 - 2 * way
        piece = ring(sign * (4 - step))
        for sub in range(3 * half, 3 * half + 3):
            value = part[piece, pl.ds(SUB * sub, SUB), :]
            if not fresh:
                last = where[way, step - 1, sub]
                wait(rcv.at[last], r_recv.at[last])
                value = value + rcv[last].astype(F32)
            now = where[way, step, sub]
            snd[now] = value.astype(BF)
            remote(
                snd.at[now], rcv.at[now], r_send, r_recv.at[now], (ring(sign) * NX + x, dp)
            ).start()

    multiply(0)
    hop(1, 0, 0, True)
    hop(0, 1, 0, True)
    arrive(1, 0)
    arrive(1, 2)
    multiply(1)
    hop(0, 0, 1, True)
    hop(1, 1, 1, True)
    for step in range(1, 4):
        for way in (1, 0):
            hop(way, step, 1 - way, False)
        if step < 3:
            for way in (0, 1):
                hop(way, step + 1, way, False)
    pending.append(lambda: wait(snd, r_send))
    for sub in range(6):
        value = part[y, pl.ds(SUB * sub, SUB), :]
        for way in range(2):
            last = where[way, 3, sub]
            wait(rcv.at[last], r_recv.at[last])
            value = value + rcv[last].astype(F32)
        value = value.astype(BF).reshape(5, 16, 128)
        for i in range(5):
            k = 5 * sub + i
            summed[lax.rem(NB * dp + k, NE), k // NE] = value[i]

    for i in (2, 1, 3, 0):
        for s in range(2):
            for k in range(2):
                column = lax.rem(x + i, NX)
                target = 2 * (2 * crow + s) + k
                tile = 2 * (4 * s + column) + k
                here = target == dp if i == 0 else False

                def local(tile=tile):
                    pltpu.make_async_copy(
                        summed.at[tile], tiles.at[pl.ds(2 * dp, 2)], t_recv
                    ).start()

                def away(tile=tile, column=column, target=target):
                    remote(
                        summed.at[tile], tiles.at[pl.ds(2 * dp, 2)], t_send, t_recv,
                        (y * NX + column, target),
                    ).start()

                if i == 0:
                    pl.when(here)(local)
                    pl.when(jnp.logical_not(here))(away)
                else:
                    away()

    @pending.append
    def _():
        @pl.when(mine)
        def _():
            wait(summed.at[pl.ds(0, NE - 1)], t_send)

        @pl.when(jnp.logical_not(mine))
        def _():
            wait(summed, t_send)

    wait(tiles.at[pl.ds(0, 2 * NE)], t_recv)

    lanes = pl.ds(pl.multiple_of(128 * lax.rem(y, 4), 128), 128)
    rows = pl.ds(pl.multiple_of(16 * lax.div(y, 4), 16), 16)

    here = h4.at[4 * side + x, c, rows, lanes]
    table_copy.wait()
    for count, (i, k, s) in enumerate(ORDER):
        held = ring(i) * NX + lax.rem(x + k, NX)
        target = 2 * (2 * brow + s) + c
        outgoing[count] = tiles[table[s, 0, held]]

        def local(count=count):
            pltpu.make_async_copy(outgoing.at[count], here, o_recv).start()

        def away(count=count, held=held, target=target):
            remote(outgoing.at[count], here, o_send, o_recv, (held, target)).start()

        if i == 0 and k == 0:
            pl.when(side == s)(local)
            pl.when(side != s)(away)
        else:
            away()

    pending.append(lambda: wait(outgoing.at[pl.ds(0, SLOTS - 1)], o_send))
    wait(h4.at[:, 0], o_recv)
    swap = remote(h4.at[:, c], h4.at[:, c], h_send, h_recv, sibling)
    swap.start()
    pending.append(swap.wait_send)
    stat_copy.wait()
    swap.wait_recv()

    block = h4[...].reshape(BS, BS)

    @pl.when(c == 0)
    def _():
        work[...] = dot(block, block, TN)

    @pl.when(c != 0)
    def _():
        work[...] = dot(block, block, NT)

    factor = STAT_DECAY * stat[...] + (1.0 - STAT_DECAY) * work[...]
    eye = lax.broadcasted_iota(jnp.int32, (BS, BS), 0) == lax.broadcasted_iota(
        jnp.int32, (BS, BS), 1
    )
    scale = jnp.sum(jnp.where(eye, factor, 0.0)) / BS + EPSILON
    first = (jnp.where(eye, 5.0, 0.0) - factor / scale) / 4.0
    pieces = split(first)
    square = exact_product(pieces, pieces)
    pieces = split(square)
    fourth = exact_product(pieces, pieces)
    moved = exact_product(split(fourth), split(5.0 * first - 4.0 * square))
    rt[c] = ((5.0 * first - moved) / 4.0).astype(BF)
    roots = remote(rt.at[c], rt.at[c], q_send, q_recv, sibling)
    roots.start()
    pending.append(roots.wait_send)
    wide = block.astype(F32)
    grad_scale = jnp.sqrt(jnp.sum(wide * wide) / (BS * BS) + EPSILON)
    roots.wait_recv()

    carried = dot(rt[0], block, NT).astype(BF)
    whole = dot(carried, rt[1])
    prec_scale = jnp.sqrt(jnp.sum(whole * whole) / (BS * BS) + EPSILON)
    res[...] = (whole * (grad_scale / prec_scale)).astype(BF).reshape(4, 128, BS)
    last = remote(res.at[2 * (1 - side) + c], got, u_send, u_recv, pair)
    last.start()
    pending.append(last.wait_send)
    out[0, 0, side] = res[2 * side + c]
    last.wait_recv()
    out[0, 0, 1 - side] = got[...]

    for done in pending:
        done()


def shards(acts, grads_out, stats, owner, col_index):
    dma = pltpu.SemaphoreType.DMA
    smem = pl.BlockSpec(memory_space=pltpu.SMEM)
    vmem = pl.BlockSpec(memory_space=pltpu.VMEM)
    return pl.pallas_call(
        kernel,
        out_shape=jax.ShapeDtypeStruct((1, 1, 2, 128, BS), BF),
        in_specs=[
            smem, smem, vmem, vmem, pl.BlockSpec(memory_space=pl.ANY)
        ],
        out_specs=vmem,
        scratch_shapes=[
            pltpu.VMEM((NX, COLS, TOK), BF),
            pltpu.VMEM((NX, 2, 2, TOK, 128), BF),
            pltpu.VMEM((NY, 2 * HALF, 128), F32),
            pltpu.VMEM((HOPS, SUB, 128), BF),
            pltpu.VMEM((HOPS, SUB, 128), BF),
            pltpu.VMEM((NE, 2, 16, 128), BF),
            pltpu.VMEM((2 * NE + 1, 16, 128), BF),
            pltpu.VMEM((SLOTS, 16, 128), BF),
            pltpu.VMEM((NZ, 2, 32, BS), BF),
            pltpu.VMEM((2, BS, BS), BF),
            pltpu.VMEM((BS, BS), F32),
            pltpu.VMEM((BS, BS), F32),
            pltpu.VMEM((4, 128, BS), BF),
            pltpu.VMEM((128, BS), BF),
            pltpu.VMEM((2, 8, 128), jnp.int32),
            pltpu.SMEM((2, 8, 128), jnp.int32),
            dma((2, 3)), dma((2, 3)), dma(()), dma(()), dma(()), dma(()),
            dma(()), dma((HOPS,)), dma(()), dma(()),
            dma(()), dma(()), dma(()), dma(()), dma(()), dma(()), dma(()), dma(()), dma(()), dma(()),
        ],
        compiler_params=pltpu.CompilerParams(
            collective_id=0, has_side_effects=True, vmem_limit_bytes=60 * 1024 * 1024
        ),
    )(owner.reshape(-1), col_index, acts, grads_out.T, stats.reshape(BS, BS))


def solution(mesh):
    return jax.shard_map(
        shards,
        mesh=mesh,
        in_specs=(P("own", "dp"), P("own", "dp"), P("own", "dp", None, None, None), P(), P()),
        out_specs=P("own", "dp", None, None, None),
        check_vma=False,
    )
```

time: 91.6 us -> 74.1 us (0.81)
  Pallas kernels: 84.7 us -> 72.3 us
  local copies, waits for them, and re-layouts: 4.81 us -> 1.67 us
  other arithmetic: 1.48 us -> 0 us
    pallas_call x1, Pallas kernels: 84.7 us -> 72.3 us  [shards(): pl.pallas_call(kernel, out_shape=jax.ShapeDtypeStruct((1, 1, 2, 128, BS),...]
    unnamed x11 -> x1, local copies, waits for them, and re-layouts: 4.26 us -> 1.67 us
where the time goes in v2:
time: 74.1 us; the launch traced here: 74 us
  Pallas kernels  72.3 us (98%)
  local copies, waits for them, and re-layouts  1.67 us (2%)
    pallas_call x1, Pallas kernels, shards(): pl.pallas_call(kernel, out_shape=jax.ShapeDtypeStruct((1, 1, 2, 128, BS),...  72.3 us
    unnamed x1, local copies, waits for them, and re-layouts  1.67 us

profile of v2, /device:TPU:1, one launch (start us, length us, event | category | flops | bytes accessed | tf_op | source)
XLA Modules:
  0.0 74.0 jit_solution(4090223166532247477)
XLA Ops:
  0.0 72.3 %shard_map.55 = bf16[1,1,2,128,512]{4,3,2,1,0:T(8,128)(2,1)} custom-call(s32[120]{0:T(128)} %bitcast.5, s32[4,30]{1,0:T(4,128)} %col_index.1, bf16[128,128]{1,0:T(8,128)(2,1)} %acts.1, bf16[960,128]{1,0:T(8,128)(2,1)} %bitcast.4, f32[512,512]{1,0:T(8,128)} %bitcast.3), custom_call_target="tpu_custom_call" | custom-call | tf_op jit(solution)/shard_map/pallas_call | solution.py:357
  72.3 1.7 %copy.7 = bf16[1,1,2,128,512]{4,3,2,1,0:T(8,128)(2,1)} copy(bf16[1,1,2,128,512]{4,3,2,1,0:T(8,128)(2,1)} %shard_map.55) | data formatting | bytes 524288

commit v3 on v2

--- a/solution.py
+++ b/solution.py
@@ -14,7 +14,6 @@
 NE = 2 * NZ
 BS = 512
 TOK = 128
-COLS = 960
 HALF = 240
 SUB = 80
 HOPS = 42
@@ -49,9 +48,9 @@
 
 def kernel(
     owner, col_index, acts, grads, stats, out,
-    bt, am, part, snd, rcv, summed, tiles, outgoing, h4, rt, stat, work, res, got, slots, table,
+    ax, bt, am, part, snd, rcv, summed, tiles, outgoing, h4, rt, stat, work, res, slots, table,
     b_send, b_recv, a_send, a_recv, f_send, f_recv, r_send, r_recv, t_send, t_recv,
-    o_send, o_recv, h_send, h_recv, q_send, q_recv, u_send, u_recv, s_sem, g_sem,
+    o_send, o_recv, h_send, h_recv, q_send, q_recv, u_send, u_recv, s_sem, g_sem, i_sem, w_sem, know,
 ):
     own = lax.axis_index("own")
     dp = lax.axis_index("dp")
@@ -76,30 +75,39 @@
 
     pending = []
 
+    barrier = pltpu.get_barrier_semaphore()
+
+    def say(sem, device):
+        pl.semaphore_signal(sem, inc=1, device_id=device, device_id_type=MESH)
+
+    def along_x(step):
+        return (y * NX + lax.rem(x + step + NX, NX), dp)
+
+    def along_z(step):
+        return (own, 2 * lax.rem(z + step + NZ, NZ) + c)
+
+    for i in (1, 2, 3):
+        say(barrier, along_x(i))
+    for i in (1, -1):
+        say(barrier, (ring(i) * NX + x, dp))
+        for k in range(NX):
+            say(barrier, (along_x(k)[0], along_z(i)[1]))
+    say(barrier, sibling)
+
+    acts_copy = pltpu.make_async_copy(acts, ax, i_sem.at[4])
+    acts_copy.start()
+    grads_copies = [
+        pltpu.make_async_copy(
+            grads.at[pl.ds(15 * g, 15), h], bt.at[x, pl.ds(15 * (2 * g + h), 15)],
+            i_sem.at[2 * g + h],
+        )
+        for g in range(2)
+        for h in range(2)
+    ]
+    for copy in grads_copies:
+        copy.start()
     stat_copy = pltpu.make_async_copy(stats, stat, s_sem)
     stat_copy.start()
-
-    barrier = pltpu.get_barrier_semaphore()
-
-    def greet(device):
-        pl.semaphore_signal(barrier, inc=1, device_id=device, device_id_type=MESH)
-
-    for i in (1, -1):
-        greet((y * NX + lax.rem(x + i + NX, NX), dp))
-        greet((ring(i) * NX + x, dp))
-    greet(sibling)
-    for i in range(NX):
-        for s in range(2):
-            @pl.when(jnp.logical_not(jnp.logical_and(x == i, z == 2 * crow + s)))
-            def _():
-                greet((y * NX + i, 2 * (2 * crow + s) + c))
-
-    turned = grads[...].reshape(NB, 2, 16, TOK)
-    for g in range(2):
-        for h in range(2):
-            bt[x, pl.ds(HALF * (2 * g + h), HALF), :] = turned[15 * g : 15 * g + 15, h].reshape(
-                HALF, TOK
-            )
     summed[...] = jnp.zeros_like(summed)
     tiles[2 * NE] = jnp.zeros((16, 128), BF)
 
@@ -122,59 +130,71 @@
     table_copy = pltpu.make_async_copy(slots, table, g_sem)
     table_copy.start()
 
-    pl.semaphore_wait(barrier, 5 + NZ - mine.astype(jnp.int32))
-
-    for i in range(NZ):
-        here = jnp.logical_and(mine, z == i)
-
-        @pl.when(here)
-        def _():
-            pltpu.make_async_copy(acts, am.at[x, side, c], a_recv).start()
-
-        @pl.when(jnp.logical_not(here))
-        def _():
+    acts_copy.wait()
+    for copy in grads_copies:
+        copy.wait()
+    pl.semaphore_wait(barrier, 14)
+    for i in (1, -1):
+        say(know.at[0], along_z(i))
+
+    def pass_on(shard, g, way, kind):
+        there = bt.at[shard, pl.ds(30 * g, 30)]
+        copy = remote(
+            there, there, b_send.at[g, kind], b_recv.at[g, kind], along_x(1 - 2 * way)
+        )
+        copy.start()
+        pending.append(copy.wait_send)
+
+    def arrive(g, kind):
+        shard = lax.rem(x + (NX - 1, 1, 2)[kind], NX)
+        wait(bt.at[shard, pl.ds(30 * g, 30)], b_recv.at[g, kind])
+        return shard
+
+    for g in range(2):
+        for way in range(2):
+            pass_on(x, g, way, way)
+
+    pl.semaphore_wait(know.at[0], 2)
+    for i in (2, -2):
+        say(know.at[1], along_z(i))
+    pl.semaphore_wait(know.at[1], 2)
+    for i in (4, 3, 5, 2, 6, 1, 7, 0):
+        plane = lax.rem(z + i, NZ)
+        column = lax.rem(brow - plane + 2 * NX, NX)
+
+        def local():
+            pltpu.make_async_copy(ax, am.at[x, side, c], a_recv).start()
+
+        def away(plane=plane, column=column):
             remote(
-                acts, am.at[x, side, c], a_send, a_recv,
-                (y * NX + lax.rem(brow - i + 2 * NX, NX), 2 * i + c),
+                ax, am.at[x, side, c], a_send, a_recv, (y * NX + column, 2 * plane + c)
             ).start()
+
+        if i == 0:
+            pl.when(mine)(local)
+            pl.when(jnp.logical_not(mine))(away)
+        else:
+            away()
+    pass_on(arrive(0, 0), 0, 0, 2)
+    pass_on(arrive(1, 1), 1, 1, 2)
 
     @pending.append
     def _():
         @pl.when(mine)
         def _():
-            wait(bt.at[0, pl.ds(0, 7 * 128)], a_send)
+            wait(bt.at[0, pl.ds(0, 56)], a_send)
 
         @pl.when(jnp.logical_not(mine))
         def _():
             wait(am.at[:, :, 0], a_send)
-
-    def pass_on(shard, g, way, kind):
-        there = bt.at[shard, pl.ds(2 * HALF * g, 2 * HALF)]
-        copy = remote(
-            there, there, b_send.at[g, kind], b_recv.at[g, kind],
-            (y * NX + lax.rem(x + (1 if way == 0 else NX - 1), NX), dp),
-        )
-        copy.start()
-        pending.append(copy.wait_send)
-
-    def arrive(g, kind):
-        shard = lax.rem(x + (NX - 1, 1, 2)[kind], NX)
-        wait(bt.at[shard, pl.ds(2 * HALF * g, 2 * HALF)], b_recv.at[g, kind])
-        return shard
-
-    for g in range(2):
-        for way in range(2):
-            pass_on(x, g, way, way)
-    pass_on(arrive(0, 0), 0, 0, 2)
-    pass_on(arrive(1, 1), 1, 1, 2)
 
     wait(am.at[:, :, 0], a_recv)
     forward = remote(am.at[:, :, c], am.at[:, :, c], f_send, f_recv, sibling)
     forward.start()
     pending.append(forward.wait_send)
-    forward.wait_recv()
     arrive(0, 1)
     arrive(0, 2)
+    forward.wait_recv()
 
     right = jnp.concatenate(
         [
@@ -185,8 +205,10 @@
     )
     def multiply(g):
         for h in range(2):
-            rows = pl.ds(HALF * (2 * g + h), HALF)
-            left = jnp.concatenate([bt[i, rows, :] for i in range(NX)], axis=1)
+            rows = pl.ds(15 * (2 * g + h), 15)
+            left = jnp.concatenate(
+                [bt[i, rows].reshape(HALF, TOK) for i in range(NX)], axis=1
+            )
             product = dot(left, right)
             for k in range(4):
                 part[4 * h + k, pl.ds(HALF * g, HALF), :] = product[:, 128 * k : 128 * k + 128]
@@ -339,12 +361,13 @@
     whole = dot(carried, rt[1])
     prec_scale = jnp.sqrt(jnp.sum(whole * whole) / (BS * BS) + EPSILON)
     res[...] = (whole * (grad_scale / prec_scale)).astype(BF).reshape(4, 128, BS)
-    last = remote(res.at[2 * (1 - side) + c], got, u_send, u_recv, pair)
+    keep = pltpu.make_async_copy(res.at[2 * side + c], out.at[0, 0, side], w_sem)
+    last = remote(res.at[2 * (1 - side) + c], out.at[0, 0, side], u_send, u_recv, pair)
     last.start()
+    keep.start()
     pending.append(last.wait_send)
-    out[0, 0, side] = res[2 * side + c]
+    pending.append(keep.wait)
     last.wait_recv()
-    out[0, 0, 1 - side] = got[...]
 
     for done in pending:
         done()
@@ -353,16 +376,17 @@
 def shards(acts, grads_out, stats, owner, col_index):
     dma = pltpu.SemaphoreType.DMA
     smem = pl.BlockSpec(memory_space=pltpu.SMEM)
-    vmem = pl.BlockSpec(memory_space=pltpu.VMEM)
+    hbm = pl.BlockSpec(memory_space=pl.ANY)
     return pl.pallas_call(
         kernel,
         out_shape=jax.ShapeDtypeStruct((1, 1, 2, 128, BS), BF),
         in_specs=[
-            smem, smem, vmem, vmem, pl.BlockSpec(memory_space=pl.ANY)
+            smem, smem, hbm, hbm, hbm
         ],
-        out_specs=vmem,
+        out_specs=hbm,
         scratch_shapes=[
-            pltpu.VMEM((NX, COLS, TOK), BF),
+            pltpu.VMEM((TOK, 128), BF),
+            pltpu.VMEM((NX, 2 * NB, 16, TOK), BF),
             pltpu.VMEM((NX, 2, 2, TOK, 128), BF),
             pltpu.VMEM((NY, 2 * HALF, 128), F32),
             pltpu.VMEM((HOPS, SUB, 128), BF),
@@ -375,17 +399,17 @@
             pltpu.VMEM((BS, BS), F32),
             pltpu.VMEM((BS, BS), F32),
             pltpu.VMEM((4, 128, BS), BF),
-            pltpu.VMEM((128, BS), BF),
             pltpu.VMEM((2, 8, 128), jnp.int32),
             pltpu.SMEM((2, 8, 128), jnp.int32),
             dma((2, 3)), dma((2, 3)), dma(()), dma(()), dma(()), dma(()),
             dma(()), dma((HOPS,)), dma(()), dma(()),
             dma(()), dma(()), dma(()), dma(()), dma(()), dma(()), dma(()), dma(()), dma(()), dma(()),
+            dma((5,)), dma(()), pltpu.SemaphoreType.REGULAR((2,)),
         ],
         compiler_params=pltpu.CompilerParams(
             collective_id=0, has_side_effects=True, vmem_limit_bytes=60 * 1024 * 1024
         ),
-    )(owner.reshape(-1), col_index, acts, grads_out.T, stats.reshape(BS, BS))
+    )(owner.reshape(-1), col_index, acts, grads_out.T.reshape(NB, 2, 16, TOK), stats.reshape(BS, BS))
 
 
 def solution(mesh):

time: 74.1 us -> 72.2 us (0.974)
  Pallas kernels: 72.3 us -> 70.4 us
    pallas_call x1, Pallas kernels: 72.3 us -> 70.4 us  [shards(): pl.pallas_call(kernel, out_shape=jax.ShapeDtypeStruct((1, 1, 2, 128, BS),...]
where the time goes in v3:
time: 72.2 us; the launch traced here: 72 us
  Pallas kernels  70.4 us (98%)
  local copies, waits for them, and re-layouts  1.67 us (2%)
    pallas_call x1, Pallas kernels, shards(): pl.pallas_call(kernel, out_shape=jax.ShapeDtypeStruct((1, 1, 2, 128, BS),...  70.4 us
    unnamed x1, local copies, waits for them, and re-layouts  1.67 us

profile of v3, /device:TPU:1, one launch (start us, length us, event | category | flops | bytes accessed | tf_op | source)
XLA Modules:
  0.0 72.0 jit_solution(7000764269150106124)
XLA Ops:
  0.0 70.4 %shard_map.55 = bf16[1,1,2,128,512]{4,3,2,1,0:T(8,128)(2,1)} custom-call(s32[120]{0:T(128)} %bitcast.7, s32[4,30]{1,0:T(4,128)} %col_index.1, bf16[128,128]{1,0:T(8,128)(2,1)} %acts.1, bf16[30,2,16,128]{3,2,1,0:T(8,128)(2,1)} %bitcast.6, f32[512,512]{1,0:T(8,128)} %bitcast.5), custom_call_target="tpu_custom_call" | custom-call | tf_op jit(solution)/shard_map/pallas_call | solution.py:380
  70.4 1.7 %copy.7 = bf16[1,1,2,128,512]{4,3,2,1,0:T(8,128)(2,1)} copy(bf16[1,1,2,128,512]{4,3,2,1,0:T(8,128)(2,1)} %shard_map.55) | data formatting | bytes 524288

commit v4 on v3

--- a/solution.py
+++ b/solution.py
@@ -32,16 +32,6 @@
     return lax.dot_general(a, b, dims, preferred_element_type=F32)
 
 
-def split(a):
-    high = a.astype(BF)
-    return high, (a - high.astype(F32)).astype(BF)
-
-
-def exact_product(a, b):
-    (ah, al), (bh, bl) = a, b
-    return dot(ah, bh) + (dot(ah, bl) + dot(al, bh))
-
-
 def wait(ref, sem):
     pltpu.make_async_copy(ref, ref, sem).wait()
 
@@ -92,6 +82,7 @@
         say(barrier, (ring(i) * NX + x, dp))
         for k in range(NX):
             say(barrier, (along_x(k)[0], along_z(i)[1]))
+            say(barrier, (along_x(k)[0], along_z(2 * i)[1]))
     say(barrier, sibling)
 
     acts_copy = pltpu.make_async_copy(acts, ax, i_sem.at[4])
@@ -133,9 +124,9 @@
     acts_copy.wait()
     for copy in grads_copies:
         copy.wait()
-    pl.semaphore_wait(barrier, 14)
-    for i in (1, -1):
-        say(know.at[0], along_z(i))
+    pl.semaphore_wait(barrier, 22)
+    for i in (2, -2):
+        say(know, along_z(i))
 
     def pass_on(shard, g, way, kind):
         there = bt.at[shard, pl.ds(30 * g, 30)]
@@ -154,20 +145,17 @@
         for way in range(2):
             pass_on(x, g, way, way)
 
-    pl.semaphore_wait(know.at[0], 2)
-    for i in (2, -2):
-        say(know.at[1], along_z(i))
-    pl.semaphore_wait(know.at[1], 2)
+    pl.semaphore_wait(know, 2)
     for i in (4, 3, 5, 2, 6, 1, 7, 0):
         plane = lax.rem(z + i, NZ)
         column = lax.rem(brow - plane + 2 * NX, NX)
 
         def local():
-            pltpu.make_async_copy(ax, am.at[x, side, c], a_recv).start()
+            pltpu.make_async_copy(ax, am.at[x, side, c], a_recv.at[side]).start()
 
         def away(plane=plane, column=column):
             remote(
-                ax, am.at[x, side, c], a_send, a_recv, (y * NX + column, 2 * plane + c)
+                ax, am.at[x, side, c], a_send, a_recv.at[side], (y * NX + column, 2 * plane + c)
             ).start()
 
         if i == 0:
@@ -188,13 +176,18 @@
         def _():
             wait(am.at[:, :, 0], a_send)
 
-    wait(am.at[:, :, 0], a_recv)
-    forward = remote(am.at[:, :, c], am.at[:, :, c], f_send, f_recv, sibling)
-    forward.start()
-    pending.append(forward.wait_send)
+    forwards = []
+    for s in range(2):
+        wait(am.at[:, s, c], a_recv.at[s])
+        forwards.append(
+            remote(am.at[:, s, c], am.at[:, s, c], f_send.at[s], f_recv.at[s], sibling)
+        )
+        forwards[s].start()
+        pending.append(forwards[s].wait_send)
     arrive(0, 1)
     arrive(0, 2)
-    forward.wait_recv()
+    for copy in forwards:
+        copy.wait_recv()
 
     right = jnp.concatenate(
         [
@@ -344,18 +337,24 @@
     )
     scale = jnp.sum(jnp.where(eye, factor, 0.0)) / BS + EPSILON
     first = (jnp.where(eye, 5.0, 0.0) - factor / scale) / 4.0
-    pieces = split(first)
-    square = exact_product(pieces, pieces)
-    pieces = split(square)
-    fourth = exact_product(pieces, pieces)
-    moved = exact_product(split(fourth), split(5.0 * first - 4.0 * square))
-    rt[c] = ((5.0 * first - moved) / 4.0).astype(BF)
-    roots = remote(rt.at[c], rt.at[c], q_send, q_recv, sibling)
-    roots.start()
-    pending.append(roots.wait_send)
+    near = first.astype(BF)
+    square = dot(near, near)
+    rest = (5.0 * near.astype(F32) - 4.0 * square).astype(BF)
+    square = square.astype(BF)
+    fourth = dot(square, square).astype(BF)
+    roots = []
+    for k in range(2):
+        rows = slice(BS // 2 * k, BS // 2 * k + BS // 2)
+        moved = dot(fourth[rows], rest)
+        there = rt.at[c, pl.ds(BS // 2 * k, BS // 2)]
+        rt[c, pl.ds(BS // 2 * k, BS // 2), :] = ((5.0 * first[rows] - moved) / 4.0).astype(BF)
+        roots.append(remote(there, there, q_send.at[k], q_recv.at[k], sibling))
+        roots[k].start()
+        pending.append(roots[k].wait_send)
     wide = block.astype(F32)
     grad_scale = jnp.sqrt(jnp.sum(wide * wide) / (BS * BS) + EPSILON)
-    roots.wait_recv()
+    for copy in roots:
+        copy.wait_recv()
 
     carried = dot(rt[0], block, NT).astype(BF)
     whole = dot(carried, rt[1])
@@ -401,10 +400,10 @@
             pltpu.VMEM((4, 128, BS), BF),
             pltpu.VMEM((2, 8, 128), jnp.int32),
             pltpu.SMEM((2, 8, 128), jnp.int32),
-            dma((2, 3)), dma((2, 3)), dma(()), dma(()), dma(()), dma(()),
+            dma((2, 3)), dma((2, 3)), dma(()), dma((2,)), dma((2,)), dma((2,)),
             dma(()), dma((HOPS,)), dma(()), dma(()),
-            dma(()), dma(()), dma(()), dma(()), dma(()), dma(()), dma(()), dma(()), dma(()), dma(()),
-            dma((5,)), dma(()), pltpu.SemaphoreType.REGULAR((2,)),
+            dma(()), dma(()), dma(()), dma(()), dma((2,)), dma((2,)), dma(()), dma(()), dma(()), dma(()),
+            dma((5,)), dma(()), pltpu.SemaphoreType.REGULAR,
         ],
         compiler_params=pltpu.CompilerParams(
             collective_id=0, has_side_effects=True, vmem_limit_bytes=60 * 1024 * 1024

time: 72.2 us -> 70.6 us (0.978)
  Pallas kernels: 70.4 us -> 68.8 us
    pallas_call x1, Pallas kernels: 70.4 us -> 68.8 us  [shards(): pl.pallas_call(kernel, out_shape=jax.ShapeDtypeStruct((1, 1, 2, 128, BS),...]
where the time goes in v4:
time: 70.6 us; the launch traced here: 70.5 us
  Pallas kernels  68.8 us (97%)
  local copies, waits for them, and re-layouts  1.67 us (2%)
    pallas_call x1, Pallas kernels, shards(): pl.pallas_call(kernel, out_shape=jax.ShapeDtypeStruct((1, 1, 2, 128, BS),...  68.8 us
    unnamed x1, local copies, waits for them, and re-layouts  1.67 us

profile of v4, /device:TPU:1, one launch (start us, length us, event | category | flops | bytes accessed | tf_op | source)
XLA Modules:
  0.0 70.5 jit_solution(448100994811800746)
XLA Ops:
  0.0 68.8 %shard_map.55 = bf16[1,1,2,128,512]{4,3,2,1,0:T(8,128)(2,1)} custom-call(s32[120]{0:T(128)} %bitcast.7, s32[4,30]{1,0:T(4,128)} %col_index.1, bf16[128,128]{1,0:T(8,128)(2,1)} %acts.1, bf16[30,2,16,128]{3,2,1,0:T(8,128)(2,1)} %bitcast.6, f32[512,512]{1,0:T(8,128)} %bitcast.5), custom_call_target="tpu_custom_call" | custom-call | tf_op jit(solution)/shard_map/pallas_call | solution.py:379
  68.8 1.7 %copy.7 = bf16[1,1,2,128,512]{4,3,2,1,0:T(8,128)(2,1)} copy(bf16[1,1,2,128,512]{4,3,2,1,0:T(8,128)(2,1)} %shard_map.55) | data formatting | bytes 524288

commit v5 on v4

--- a/solution.py
+++ b/solution.py
@@ -65,26 +65,6 @@
 
     pending = []
 
-    barrier = pltpu.get_barrier_semaphore()
-
-    def say(sem, device):
-        pl.semaphore_signal(sem, inc=1, device_id=device, device_id_type=MESH)
-
-    def along_x(step):
-        return (y * NX + lax.rem(x + step + NX, NX), dp)
-
-    def along_z(step):
-        return (own, 2 * lax.rem(z + step + NZ, NZ) + c)
-
-    for i in (1, 2, 3):
-        say(barrier, along_x(i))
-    for i in (1, -1):
-        say(barrier, (ring(i) * NX + x, dp))
-        for k in range(NX):
-            say(barrier, (along_x(k)[0], along_z(i)[1]))
-            say(barrier, (along_x(k)[0], along_z(2 * i)[1]))
-    say(barrier, sibling)
-
     acts_copy = pltpu.make_async_copy(acts, ax, i_sem.at[4])
     acts_copy.start()
     grads_copies = [
@@ -99,6 +79,74 @@
         copy.start()
     stat_copy = pltpu.make_async_copy(stats, stat, s_sem)
     stat_copy.start()
+
+    barrier = pltpu.get_barrier_semaphore()
+
+    def say(sem, device):
+        pl.semaphore_signal(sem, inc=1, device_id=device, device_id_type=MESH)
+
+    def along_x(step):
+        return (y * NX + lax.rem(x + step + NX, NX), dp)
+
+    def along_z(step):
+        return (own, 2 * lax.rem(z + step + NZ, NZ) + c)
+
+    for i in (1, 2, 3):
+        say(barrier, along_x(i))
+    for i in (1, -1, 2, -2):
+        say(barrier, (ring(i) * NX + x, dp))
+    say(barrier, sibling)
+    for i in (1, -1, 2, -2):
+        for k in range(NX):
+            say(barrier, (along_x(k)[0], along_z(i)[1]))
+
+    acts_copy.wait()
+    for copy in grads_copies:
+        copy.wait()
+    pl.semaphore_wait(barrier, 24)
+    for i in (2, -2):
+        say(know, along_z(i))
+
+    def pass_on(shard, g, way, kind):
+        there = bt.at[shard, pl.ds(30 * g, 30)]
+        copy = remote(
+            there, there, b_send.at[g, kind], b_recv.at[g, kind], along_x(1 - 2 * way)
+        )
+        copy.start()
+        pending.append(copy.wait_send)
+
+    def arrive(g, kind):
+        shard = lax.rem(x + (NX - 1, 1, 2)[kind], NX)
+        wait(bt.at[shard, pl.ds(30 * g, 30)], b_recv.at[g, kind])
+        return shard
+
+    def inputs_out(i):
+        plane = lax.rem(z + i, NZ)
+        column = lax.rem(brow - plane + 2 * NX, NX)
+
+        def local():
+            pltpu.make_async_copy(ax, am.at[x, side, c], a_recv.at[side]).start()
+
+        def away(plane=plane, column=column):
+            remote(
+                ax, am.at[x, side, c], a_send, a_recv.at[side], (y * NX + column, 2 * plane + c)
+            ).start()
+
+        if i == 0:
+            pl.when(mine)(local)
+            pl.when(jnp.logical_not(mine))(away)
+        else:
+            away()
+
+    for i in (2, 6, 1, 7, 0):
+        inputs_out(i)
+    for g in range(2):
+        for way in range(2):
+            pass_on(x, (g + way) % 2, way, way)
+    pl.semaphore_wait(know, 2)
+    for i in (4, 3, 5):
+        inputs_out(i)
+
     summed[...] = jnp.zeros_like(summed)
     tiles[2 * NE] = jnp.zeros((16, 128), BF)
 
@@ -121,48 +169,6 @@
     table_copy = pltpu.make_async_copy(slots, table, g_sem)
     table_copy.start()
 
-    acts_copy.wait()
-    for copy in grads_copies:
-        copy.wait()
-    pl.semaphore_wait(barrier, 22)
-    for i in (2, -2):
-        say(know, along_z(i))
-
-    def pass_on(shard, g, way, kind):
-        there = bt.at[shard, pl.ds(30 * g, 30)]
-        copy = remote(
-            there, there, b_send.at[g, kind], b_recv.at[g, kind], along_x(1 - 2 * way)
-        )
-        copy.start()
-        pending.append(copy.wait_send)
-
-    def arrive(g, kind):
-        shard = lax.rem(x + (NX - 1, 1, 2)[kind], NX)
-        wait(bt.at[shard, pl.ds(30 * g, 30)], b_recv.at[g, kind])
-        return shard
-
-    for g in range(2):
-        for way in range(2):
-            pass_on(x, g, way, way)
-
-    pl.semaphore_wait(know, 2)
-    for i in (4, 3, 5, 2, 6, 1, 7, 0):
-        plane = lax.rem(z + i, NZ)
-        column = lax.rem(brow - plane + 2 * NX, NX)
-
-        def local():
-            pltpu.make_async_copy(ax, am.at[x, side, c], a_recv.at[side]).start()
-
-        def away(plane=plane, column=column):
-            remote(
-                ax, am.at[x, side, c], a_send, a_recv.at[side], (y * NX + column, 2 * plane + c)
-            ).start()
-
-        if i == 0:
-            pl.when(mine)(local)
-            pl.when(jnp.logical_not(mine))(away)
-        else:
-            away()
     pass_on(arrive(0, 0), 0, 0, 2)
     pass_on(arrive(1, 1), 1, 1, 2)
 
@@ -207,41 +213,41 @@
                 part[4 * h + k, pl.ds(HALF * g, HALF), :] = product[:, 128 * k : 128 * k + 128]
 
     where = {}
-    for step in range(4):
+    for stage in range(4):
         for way in range(2):
             for sub in range(6):
-                if step or sub // 3 != way:
-                    where[way, step, sub] = len(where)
-
-    def hop(way, step, half, fresh):
+                if stage or sub % 2 != way:
+                    where[way, stage, sub] = len(where)
+
+    def hop(way, stage, sub):
         sign = 1 - 2 * way
-        piece = ring(sign * (4 - step))
-        for sub in range(3 * half, 3 * half + 3):
-            value = part[piece, pl.ds(SUB * sub, SUB), :]
-            if not fresh:
-                last = where[way, step - 1, sub]
+        value = part[ring(sign * (4 - stage)), pl.ds(SUB * sub, SUB), :]
+        for last in ((0, 1) if stage == 2 else (2,) if stage == 3 else ()):
+            if (way, last, sub) in where:
+                last = where[way, last, sub]
                 wait(rcv.at[last], r_recv.at[last])
                 value = value + rcv[last].astype(F32)
-            now = where[way, step, sub]
-            snd[now] = value.astype(BF)
-            remote(
-                snd.at[now], rcv.at[now], r_send, r_recv.at[now], (ring(sign) * NX + x, dp)
-            ).start()
-
-    multiply(0)
-    hop(1, 0, 0, True)
-    hop(0, 1, 0, True)
+        now = where[way, stage, sub]
+        snd[now] = value.astype(BF)
+        target = ring(sign * (1 if stage else 2)) * NX + x
+        remote(snd.at[now], rcv.at[now], r_send, r_recv.at[now], (target, dp)).start()
+
+    def begin(g):
+        multiply(g)
+        for i in range(3 * g, 3 * g + 3):
+            hop(1 - i % 2, 0, i)
+        for i in range(3 * g, 3 * g + 3):
+            hop(1, 1, i)
+            hop(0, 1, i)
+
+    begin(0)
     arrive(1, 0)
     arrive(1, 2)
-    multiply(1)
-    hop(0, 0, 1, True)
-    hop(1, 1, 1, True)
-    for step in range(1, 4):
-        for way in (1, 0):
-            hop(way, step, 1 - way, False)
-        if step < 3:
-            for way in (0, 1):
-                hop(way, step + 1, way, False)
+    begin(1)
+    for stage in (2, 3):
+        for i in range(6):
+            hop(1, stage, i)
+            hop(0, stage, i)
     pending.append(lambda: wait(snd, r_send))
     for sub in range(6):
         value = part[y, pl.ds(SUB * sub, SUB), :]
@@ -294,32 +300,40 @@
     lanes = pl.ds(pl.multiple_of(128 * lax.rem(y, 4), 128), 128)
     rows = pl.ds(pl.multiple_of(16 * lax.div(y, 4), 16), 16)
 
-    here = h4.at[4 * side + x, c, rows, lanes]
+    here = h4.at[side, x, c, rows, lanes]
     table_copy.wait()
-    for count, (i, k, s) in enumerate(ORDER):
-        held = ring(i) * NX + lax.rem(x + k, NX)
-        target = 2 * (2 * brow + s) + c
-        outgoing[count] = tiles[table[s, 0, held]]
-
-        def local(count=count):
-            pltpu.make_async_copy(outgoing.at[count], here, o_recv).start()
-
-        def away(count=count, held=held, target=target):
-            remote(outgoing.at[count], here, o_send, o_recv, (held, target)).start()
-
-        if i == 0 and k == 0:
-            pl.when(side == s)(local)
-            pl.when(side != s)(away)
-        else:
-            away()
+    for batch in range(0, SLOTS, 16):
+        places = list(enumerate(ORDER))[batch : batch + 16]
+        held = [ring(i) * NX + lax.rem(x + k, NX) for _, (i, k, s) in places]
+        for (count, (i, k, s)), owner_id in zip(places, held):
+            outgoing[count] = tiles[table[s, 0, owner_id]]
+        for (count, (i, k, s)), owner_id in zip(places, held):
+            target = 2 * (2 * brow + s) + c
+
+            def local(count=count):
+                pltpu.make_async_copy(outgoing.at[count], here, o_recv.at[side]).start()
+
+            def away(count=count, owner_id=owner_id, target=target):
+                remote(
+                    outgoing.at[count], here, o_send, o_recv.at[side], (owner_id, target)
+                ).start()
+
+            if i == 0 and k == 0:
+                pl.when(side == s)(local)
+                pl.when(side != s)(away)
+            else:
+                away()
 
     pending.append(lambda: wait(outgoing.at[pl.ds(0, SLOTS - 1)], o_send))
-    wait(h4.at[:, 0], o_recv)
-    swap = remote(h4.at[:, c], h4.at[:, c], h_send, h_recv, sibling)
-    swap.start()
-    pending.append(swap.wait_send)
+    swaps = []
+    for s in range(2):
+        wait(h4.at[s, :, c], o_recv.at[s])
+        swaps.append(remote(h4.at[s, :, c], h4.at[s, :, c], h_send.at[s], h_recv.at[s], sibling))
+        swaps[s].start()
+        pending.append(swaps[s].wait_send)
     stat_copy.wait()
-    swap.wait_recv()
+    for copy in swaps:
+        copy.wait_recv()
 
     block = h4[...].reshape(BS, BS)
 
@@ -359,9 +373,13 @@
     carried = dot(rt[0], block, NT).astype(BF)
     whole = dot(carried, rt[1])
     prec_scale = jnp.sqrt(jnp.sum(whole * whole) / (BS * BS) + EPSILON)
-    res[...] = (whole * (grad_scale / prec_scale)).astype(BF).reshape(4, 128, BS)
-    keep = pltpu.make_async_copy(res.at[2 * side + c], out.at[0, 0, side], w_sem)
-    last = remote(res.at[2 * (1 - side) + c], out.at[0, 0, side], u_send, u_recv, pair)
+    wide_rows = BS // 4
+    work[...] = whole
+    for k in range(2):
+        quarter = pl.ds(pl.multiple_of(wide_rows * (2 * k + c), wide_rows), wide_rows)
+        res[k] = (work[quarter, :] * (grad_scale / prec_scale)).astype(BF)
+    keep = pltpu.make_async_copy(res.at[side], out.at[0, 0, side], w_sem)
+    last = remote(res.at[1 - side], out.at[0, 0, side], u_send, u_recv, pair)
     last.start()
     keep.start()
     pending.append(last.wait_send)
@@ -393,16 +411,16 @@
             pltpu.VMEM((NE, 2, 16, 128), BF),
             pltpu.VMEM((2 * NE + 1, 16, 128), BF),
             pltpu.VMEM((SLOTS, 16, 128), BF),
-            pltpu.VMEM((NZ, 2, 32, BS), BF),
+            pltpu.VMEM((2, NX, 2, 32, BS), BF),
             pltpu.VMEM((2, BS, BS), BF),
             pltpu.VMEM((BS, BS), F32),
             pltpu.VMEM((BS, BS), F32),
-            pltpu.VMEM((4, 128, BS), BF),
+            pltpu.VMEM((2, 128, BS), BF),
             pltpu.VMEM((2, 8, 128), jnp.int32),
             pltpu.SMEM((2, 8, 128), jnp.int32),
             dma((2, 3)), dma((2, 3)), dma(()), dma((2,)), dma((2,)), dma((2,)),
             dma(()), dma((HOPS,)), dma(()), dma(()),
-            dma(()), dma(()), dma(()), dma(()), dma((2,)), dma((2,)), dma(()), dma(()), dma(()), dma(()),
+            dma(()), dma((2,)), dma((2,)), dma((2,)), dma((2,)), dma((2,)), dma(()), dma(()), dma(()), dma(()),
             dma((5,)), dma(()), pltpu.SemaphoreType.REGULAR,
         ],
         compiler_params=pltpu.CompilerParams(

time: 70.6 us -> 69.5 us (0.984)
  Pallas kernels: 68.8 us -> 67.7 us
    pallas_call x1, Pallas kernels: 68.8 us -> 67.7 us  [shards(): pl.pallas_call(kernel, out_shape=jax.ShapeDtypeStruct((1, 1, 2, 128, BS),...]
where the time goes in v5:
time: 69.5 us; the launch traced here: 69.3 us
  Pallas kernels  67.7 us (97%)
  local copies, waits for them, and re-layouts  1.67 us (2%)
    pallas_call x1, Pallas kernels, shards(): pl.pallas_call(kernel, out_shape=jax.ShapeDtypeStruct((1, 1, 2, 128, BS),...  67.7 us
    unnamed x1, local copies, waits for them, and re-layouts  1.67 us

profile of v5, /device:TPU:1, one launch (start us, length us, event | category | flops | bytes accessed | tf_op | source)
XLA Modules:
  0.0 69.3 jit_solution(3445188393645407197)
XLA Ops:
  0.0 67.7 %shard_map.55 = bf16[1,1,2,128,512]{4,3,2,1,0:T(8,128)(2,1)} custom-call(s32[120]{0:T(128)} %bitcast.7, s32[4,30]{1,0:T(4,128)} %col_index.1, bf16[128,128]{1,0:T(8,128)(2,1)} %acts.1, bf16[30,2,16,128]{3,2,1,0:T(8,128)(2,1)} %bitcast.6, f32[512,512]{1,0:T(8,128)} %bitcast.5), custom_call_target="tpu_custom_call" | custom-call | tf_op jit(solution)/shard_map/pallas_call | solution.py:397
  67.7 1.7 %copy.7 = bf16[1,1,2,128,512]{4,3,2,1,0:T(8,128)(2,1)} copy(bf16[1,1,2,128,512]{4,3,2,1,0:T(8,128)(2,1)} %shard_map.55) | data formatting | bytes 524288

commit v6 on v5

--- a/solution.py
+++ b/solution.py
@@ -37,8 +37,8 @@
 
 
 def kernel(
-    owner, col_index, acts, grads, stats, out,
-    ax, bt, am, part, snd, rcv, summed, tiles, outgoing, h4, rt, stat, work, res, slots, table,
+    owner, col_index, acts, grads, stats, out, scales,
+    ax, bt, am, part, snd, rcv, summed, tiles, outgoing, h4, rt, stat, work, res, graft, slots, table,
     b_send, b_recv, a_send, a_recv, f_send, f_recv, r_send, r_recv, t_send, t_recv,
     o_send, o_recv, h_send, h_recv, q_send, q_recv, u_send, u_recv, s_sem, g_sem, i_sem, w_sem, know,
 ):
@@ -202,15 +202,17 @@
         ],
         axis=0,
     )
+
     def multiply(g):
+        left = jnp.concatenate(
+            [bt[i, pl.ds(30 * g, 30)].reshape(2 * HALF, TOK) for i in range(NX)], axis=1
+        )
+        product = dot(left, right)
         for h in range(2):
-            rows = pl.ds(15 * (2 * g + h), 15)
-            left = jnp.concatenate(
-                [bt[i, rows].reshape(HALF, TOK) for i in range(NX)], axis=1
-            )
-            product = dot(left, right)
             for k in range(4):
-                part[4 * h + k, pl.ds(HALF * g, HALF), :] = product[:, 128 * k : 128 * k + 128]
+                part[4 * h + k, pl.ds(HALF * g, HALF), :] = product[
+                    HALF * h : HALF * h + HALF, 128 * k : 128 * k + 128
+                ]
 
     where = {}
     for stage in range(4):
@@ -370,21 +372,30 @@
     for copy in roots:
         copy.wait_recv()
 
+    quarter = pl.ds(pl.multiple_of(128 * (2 * (1 - side) + c), 128), 128)
+    carried = dot(rt[0, quarter, :], block, NT).astype(BF)
+    res[1] = dot(carried, rt[1]).astype(BF)
+    last = remote(res.at[1], out.at[0, 0, side], u_send.at[0], u_recv.at[0], pair)
+    last.start()
+    pending.append(last.wait_send)
     carried = dot(rt[0], block, NT).astype(BF)
     whole = dot(carried, rt[1])
+    work[...] = whole
+    quarter = pl.ds(pl.multiple_of(128 * (2 * side + c), 128), 128)
+    res[0] = work[quarter, :].astype(BF)
+    keep = pltpu.make_async_copy(res.at[0], out.at[0, 0, side], w_sem.at[0])
+    keep.start()
+    pending.append(keep.wait)
     prec_scale = jnp.sqrt(jnp.sum(whole * whole) / (BS * BS) + EPSILON)
-    wide_rows = BS // 4
-    work[...] = whole
-    for k in range(2):
-        quarter = pl.ds(pl.multiple_of(wide_rows * (2 * k + c), wide_rows), wide_rows)
-        res[k] = (work[quarter, :] * (grad_scale / prec_scale)).astype(BF)
-    keep = pltpu.make_async_copy(res.at[side], out.at[0, 0, side], w_sem)
-    last = remote(res.at[1 - side], out.at[0, 0, side], u_send, u_recv, pair)
-    last.start()
-    keep.start()
-    pending.append(last.wait_send)
-    pending.append(keep.wait)
+    graft[...] = jnp.full(graft.shape, grad_scale / prec_scale, F32)
+    scale_out = remote(graft, scales.at[side], u_send.at[1], u_recv.at[1], pair)
+    scale_out.start()
+    pending.append(scale_out.wait_send)
+    keep_scale = pltpu.make_async_copy(graft, scales.at[side], w_sem.at[1])
+    keep_scale.start()
+    pending.append(keep_scale.wait)
     last.wait_recv()
+    scale_out.wait_recv()
 
     for done in pending:
         done()
@@ -394,13 +405,16 @@
     dma = pltpu.SemaphoreType.DMA
     smem = pl.BlockSpec(memory_space=pltpu.SMEM)
     hbm = pl.BlockSpec(memory_space=pl.ANY)
-    return pl.pallas_call(
+    raw, scales = pl.pallas_call(
         kernel,
-        out_shape=jax.ShapeDtypeStruct((1, 1, 2, 128, BS), BF),
+        out_shape=(
+            jax.ShapeDtypeStruct((1, 1, 2, 128, BS), BF),
+            jax.ShapeDtypeStruct((2, 8, BS), F32),
+        ),
         in_specs=[
             smem, smem, hbm, hbm, hbm
         ],
-        out_specs=hbm,
+        out_specs=(hbm, hbm),
         scratch_shapes=[
             pltpu.VMEM((TOK, 128), BF),
             pltpu.VMEM((NX, 2 * NB, 16, TOK), BF),
@@ -416,17 +430,20 @@
             pltpu.VMEM((BS, BS), F32),
             pltpu.VMEM((BS, BS), F32),
             pltpu.VMEM((2, 128, BS), BF),
+            pltpu.VMEM((8, BS), F32),
             pltpu.VMEM((2, 8, 128), jnp.int32),
             pltpu.SMEM((2, 8, 128), jnp.int32),
             dma((2, 3)), dma((2, 3)), dma(()), dma((2,)), dma((2,)), dma((2,)),
             dma(()), dma((HOPS,)), dma(()), dma(()),
-            dma(()), dma((2,)), dma((2,)), dma((2,)), dma((2,)), dma((2,)), dma(()), dma(()), dma(()), dma(()),
-            dma((5,)), dma(()), pltpu.SemaphoreType.REGULAR,
+            dma(()), dma((2,)), dma((2,)), dma((2,)), dma((2,)), dma((2,)), dma((2,)), dma((2,)), dma(()), dma(()),
+            dma((5,)), dma((2,)), pltpu.SemaphoreType.REGULAR,
         ],
         compiler_params=pltpu.CompilerParams(
             collective_id=0, has_side_effects=True, vmem_limit_bytes=60 * 1024 * 1024
         ),
     )(owner.reshape(-1), col_index, acts, grads_out.T.reshape(NB, 2, 16, TOK), stats.reshape(BS, BS))
+    scaled = raw.reshape(2, 16, 8, BS).astype(F32) * scales[:, None]
+    return scaled.astype(BF).reshape(raw.shape)
 
 
 def solution(mesh):

time: 69.5 us -> 69.1 us (level)
  other arithmetic: 0 us -> 1.7 us
  local copies, waits for them, and re-layouts: 1.67 us -> 0 us
  Pallas kernels: 67.7 us -> 67 us
    convert_element_type x0 -> x1, other arithmetic: none -> 1.7 us  [shards(): return scaled.astype(BF).reshape(raw.shape)]
    unnamed x1 -> x0, local copies, waits for them, and re-layouts: 1.67 us -> none
where the time goes in v6:
time: 69.1 us; the launch traced here: 68.7 us
  Pallas kernels  67 us (97%)
  other arithmetic  1.7 us (2%)
    pallas_call x1, Pallas kernels, shards(): pl.pallas_call(kernel, out_shape=(jax.ShapeDtypeStruct((1, 1, 2, 128, BS)...  67 us
    convert_element_type x1, other arithmetic, shards(): return scaled.astype(BF).reshape(raw.shape)  1.7 us

profile of v6, /device:TPU:1, one launch (start us, length us, event | category | flops | bytes accessed | tf_op | source)
XLA Modules:
  0.0 68.7 jit_solution(946125219884423515)
XLA Ops:
  0.0 67.0 %shard_map.55 = (bf16[1,1,2,128,512]{4,3,2,1,0:T(8,128)(2,1)}, f32[2,8,512]{2,1,0:T(8,128)}) custom-call(s32[120]{0:T(128)} %bitcast.11, s32[4,30]{1,0:T(4,128)} %col_index.1, bf16[128,128]{1,0:T(8,128)(2,1)} %acts.1, bf16[30,2,16,128]{3,2,1,0:T(8,128)(2,1)} %bitcast.10, f32[512,512]{1,0:T(8,128)} %bitcast.9), custom_call_target="tpu_custom_call" | custom-call | tf_op jit(solution)/shard_map/pallas_call | solution.py:408
  67.0 1.7 %fusion = bf16[1,1,2,128,512]{4,3,2,1,0:T(8,128)(2,1)} fusion(bf16[1,1,2,128,512]{4,3,2,1,0:T(8,128)(2,1)} %get-tuple-element.7, f32[2,8,512]{2,1,0:T(8,128)} %get-tuple-element.8), kind=kLoop, calls=%fused_computation.1 | loop fusion | flops 393216 | bytes 557056 | tf_op jit(solution)/shard_map/convert_element_type | solution.py:446

commit v7 on v6

--- a/solution.py
+++ b/solution.py
@@ -21,7 +21,7 @@
 SLOTS = 64
 ORDER = sorted(
     ((i, k, s) for i in range(NY) for k in range(NX) for s in range(2)),
-    key=lambda t: -min(t[0], NY - t[0]) - min(t[1], NX - t[1]),
+    key=lambda t: -min(t[0], NY - t[0]) - min(t[1], NX - t[1]) - t[2],
 )
 NN = (((1,), (0,)), ((), ()))
 NT = (((1,), (1,)), ((), ()))
@@ -308,9 +308,9 @@
         places = list(enumerate(ORDER))[batch : batch + 16]
         held = [ring(i) * NX + lax.rem(x + k, NX) for _, (i, k, s) in places]
         for (count, (i, k, s)), owner_id in zip(places, held):
-            outgoing[count] = tiles[table[s, 0, owner_id]]
+            outgoing[count] = tiles[table[1 - side if s else side, 0, owner_id]]
         for (count, (i, k, s)), owner_id in zip(places, held):
-            target = 2 * (2 * brow + s) + c
+            target = pair[1] if s else dp
 
             def local(count=count):
                 pltpu.make_async_copy(outgoing.at[count], here, o_recv.at[side]).start()
@@ -320,9 +320,8 @@
                     outgoing.at[count], here, o_send, o_recv.at[side], (owner_id, target)
                 ).start()
 
-            if i == 0 and k == 0:
-                pl.when(side == s)(local)
-                pl.when(side != s)(away)
+            if (i, k, s) == (0, 0, 0):
+                local()
             else:
                 away()
 

time: 69.1 us -> 68.6 us (level)
  no operation moved by 1% of the time
where the time goes in v7:
time: 68.6 us; the launch traced here: 68.2 us
  Pallas kernels  66.4 us (97%)
  other arithmetic  1.7 us (2%)
    pallas_call x1, Pallas kernels, shards(): pl.pallas_call(kernel, out_shape=(jax.ShapeDtypeStruct((1, 1, 2, 128, BS)...  66.4 us
    convert_element_type x1, other arithmetic, shards(): return scaled.astype(BF).reshape(raw.shape)  1.7 us

profile of v7, /device:TPU:1, one launch (start us, length us, event | category | flops | bytes accessed | tf_op | source)
XLA Modules:
  0.0 68.2 jit_solution(8581978159626308507)
XLA Ops:
  0.0 66.4 %shard_map.55 = (bf16[1,1,2,128,512]{4,3,2,1,0:T(8,128)(2,1)}, f32[2,8,512]{2,1,0:T(8,128)}) custom-call(s32[120]{0:T(128)} %bitcast.11, s32[4,30]{1,0:T(4,128)} %col_index.1, bf16[128,128]{1,0:T(8,128)(2,1)} %acts.1, bf16[30,2,16,128]{3,2,1,0:T(8,128)(2,1)} %bitcast.10, f32[512,512]{1,0:T(8,128)} %bitcast.9), custom_call_target="tpu_custom_call" | custom-call | tf_op jit(solution)/shard_map/pallas_call | solution.py:407
  66.5 1.7 %fusion = bf16[1,1,2,128,512]{4,3,2,1,0:T(8,128)(2,1)} fusion(bf16[1,1,2,128,512]{4,3,2,1,0:T(8,128)(2,1)} %get-tuple-element.7, f32[2,8,512]{2,1,0:T(8,128)} %get-tuple-element.8), kind=kLoop, calls=%fused_computation.1 | loop fusion | flops 393216 | bytes 557056 | tf_op jit(solution)/shard_map/convert_element_type | solution.py:445
